TPU v7x, 32 devices: a whole 2x2x4 slice. The times are simulated.
32 devices in a mesh: dp: 16 (over z, y, x), tensor: 2 (over core).
Axes of the slice: x: 2, y: 2, z: 4, core: 2. Of those that a mesh axis runs over, the one named last changes fastest.
Arguments:
- tokens: bfloat16 [16384, 768], P('dp'), may hold values from -6 to 6
- positions: int32 [16384], P('dp'), may hold values from 0 to 1023, as said below
- norm_gain: float32 [2, 2, 768], replicated, may hold values from 0.25 to 1.75
- norm_shift: float32 [2, 2, 768], replicated, may hold values from -1.8 to 1.8
- heads_weight: bfloat16 [2, 3, 768, 768], P(None, None, None, 'tensor'), may hold values from -0.21875 to 0.21875
- offsets: float32 [2, 2, 768], P(None, None, 'tensor'), may hold values from -3 to 3
- merge_weight: bfloat16 [2, 768, 768], P(None, 'tensor'), may hold values from -0.875 to 0.875
- branch_bias: float32 [2, 2, 768], replicated, may hold values from -3 to 3
- expand_weight: bfloat16 [2, 768, 3072], P(None, None, 'tensor'), may hold values from -0.21875 to 0.21875
- hidden_bias: float32 [2, 3072], P(None, 'tensor'), may hold values from -3 to 3
- shrink_weight: bfloat16 [2, 3072, 768], P(None, 'tensor'), may hold values from -0.109375 to 0.109375
- cotangent: bfloat16 [16384, 768], P('dp'), may hold values from -6 to 6
Outputs:
- output: bfloat16 [16384, 768], P('dp')
- grad_tokens: bfloat16 [16384, 768], P('dp')
- grad_gain: float32 [2, 2, 768], replicated
- grad_shift: float32 [2, 2, 768], replicated
- grad_heads: float32 [2, 3, 768, 768], P(None, None, None, 'tensor')
- grad_offsets: float32 [2, 2, 768], P(None, None, 'tensor')
- grad_merge: float32 [2, 768, 768], P(None, 'tensor')
- grad_branch: float32 [2, 2, 768], replicated
- grad_expand: float32 [2, 768, 3072], P(None, None, 'tensor')
- grad_hidden: float32 [2, 3072], P(None, 'tensor')
- grad_shrink: float32 [2, 3072, 768], P(None, 'tensor')
Inputs may be any that keep to these rules, and one draw needn't show every extreme that they name: `positions`: each sequence of 1024 tokens is packed documents: a value counts up by one from 0 at each document's first token; sequence 0 is a single document.
All inputs are finite; a program needn't handle non-finite values.
Results may differ from a plain program's by a relative error of at most 0.018.
Values sent between devices are 32-bit elements; how exact they have to be, the bound alone decides.
A program may use at most 256 MiB of HBM per device.

v0:
```python
import jax
import jax.numpy as jnp
from jax import lax
from jax.sharding import PartitionSpec as P

HEAD_DIM = 64
LEN = 1024
LAYERS = 2


def layer_norm(stream, gain_row, shift_row):
    centre = stream - jnp.mean(stream, axis=-1, keepdims=True)
    spread = jnp.mean(centre * centre, axis=-1, keepdims=True)
    return centre * lax.rsqrt(spread + 1e-05) * gain_row + shift_row


def gelu_tanh(values):
    return (
        0.5
        * values
        * (1.0 + jnp.tanh(0.7978845608028654 * (values + 0.044715 * values * values * values)))
    )


def block_mask(first_row, amount, offset_part, length):
    query_index = first_row + jnp.arange(amount, dtype=jnp.int32)
    key_index = jnp.arange(length, dtype=jnp.int32)
    return (key_index[None, :] <= query_index[:, None]) & (
        key_index[None, :] >= (query_index - offset_part)[:, None]
    )


def attend_sequence(query_rows, key_rows, value_rows, offsets_row):
    length = query_rows.shape[0]
    local_heads = query_rows.shape[1]
    stride = min(512, length)
    pieces = length // stride

    def one_block(record):
        position, query_part, offset_part = record
        scores = (
            jnp.einsum("qhd,khd->hqk", query_part, key_rows, preferred_element_type=jnp.float32)
            * 0.125
        )
        allowed = block_mask(position * stride, stride, offset_part, length)
        scores = jnp.where(allowed[None], scores, -1e30)
        highest = jnp.max(scores, axis=-1, keepdims=True)
        weights = jnp.exp(scores - highest)
        totals = jnp.sum(weights, axis=-1, keepdims=True)
        chances = (weights / totals).astype(jnp.bfloat16)
        blended = jnp.einsum(
            "hqk,khd->qhd", chances, value_rows, preferred_element_type=jnp.float32
        )
        return (blended.astype(jnp.bfloat16), (highest + jnp.log(totals))[:, :, 0])

    blended, logsum = lax.map(
        one_block,
        (
            jnp.arange(pieces, dtype=jnp.int32),
            query_rows.reshape(pieces, stride, local_heads, HEAD_DIM),
            offsets_row.reshape(pieces, stride),
        ),
    )
    return (blended.reshape(length, local_heads, HEAD_DIM), logsum)


def attend_back(query_rows, key_rows, value_rows, offsets_row, logsum, grad_blended):
    length = query_rows.shape[0]
    local_heads = query_rows.shape[1]
    stride = min(512, length)
    pieces = length // stride

    def one_block(running, record):
        grad_keys, grad_values = running
        position, query_part, offset_part, logsum_part, grad_part = record
        scores = (
            jnp.einsum("qhd,khd->hqk", query_part, key_rows, preferred_element_type=jnp.float32)
            * 0.125
        )
        allowed = block_mask(position * stride, stride, offset_part, length)
        chances = jnp.where(allowed[None], jnp.exp(scores - logsum_part[:, :, None]), 0.0)
        grad_chances = jnp.einsum(
            "qhd,khd->hqk", grad_part, value_rows, preferred_element_type=jnp.float32
        )
        centre = jnp.sum(chances * grad_chances, axis=-1, keepdims=True)
        grad_scores = (chances * (grad_chances - centre)).astype(jnp.bfloat16)
        grad_query = (
            jnp.einsum("hqk,khd->qhd", grad_scores, key_rows, preferred_element_type=jnp.float32)
            * 0.125
        )
        grad_keys = (
            grad_keys
            + jnp.einsum(
                "hqk,qhd->khd", grad_scores, query_part, preferred_element_type=jnp.float32
            )
            * 0.125
        )
        grad_values = grad_values + jnp.einsum(
            "hqk,qhd->khd",
            chances.astype(jnp.bfloat16),
            grad_part,
            preferred_element_type=jnp.float32,
        )
        return ((grad_keys, grad_values), grad_query.astype(jnp.bfloat16))

    empty = jnp.zeros((length, local_heads, HEAD_DIM), jnp.float32)
    (grad_keys, grad_values), grad_query = lax.scan(
        one_block,
        (empty, empty),
        (
            jnp.arange(pieces, dtype=jnp.int32),
            query_rows.reshape(pieces, stride, local_heads, HEAD_DIM),
            offsets_row.reshape(pieces, stride),
            logsum,
            grad_blended.reshape(pieces, stride, local_heads, HEAD_DIM),
        ),
    )
    return (
        grad_query.reshape(length, local_heads, HEAD_DIM),
        grad_keys.astype(jnp.bfloat16),
        grad_values.astype(jnp.bfloat16),
    )


def add_branch(stream, partial_sum, bias_row):
    return stream + (lax.psum(partial_sum, "tensor") + bias_row)


def reduce_inputs(partial_sum):
    return lax.psum(partial_sum, "tensor")


def reduce_grads(gradients):
    flattened = tuple((member.reshape(-1) for member in gradients))
    shares = lax.psum_scatter(flattened, "dp", scatter_dimension=0, tiled=True)
    summed = lax.all_gather(shares, "dp", axis=0, tiled=True)
    return tuple((whole.reshape(member.shape) for whole, member in zip(summed, gradients)))


def to_heads(matrix, sequences, local_heads):
    return matrix.reshape(sequences, LEN, local_heads, HEAD_DIM)


def on_device(
    tokens,
    positions,
    norm_gain,
    norm_shift,
    heads_weight,
    offsets,
    merge_weight,
    branch_bias,
    expand_weight,
    hidden_bias,
    shrink_weight,
    cotangent,
):
    row_count = tokens.shape[0]
    local_width = heads_weight.shape[3]
    local_heads = local_width // HEAD_DIM
    sequences = row_count // LEN
    offsets_rows = positions.reshape(sequences, LEN)
    stream = tokens.astype(jnp.float32)
    kept_values = []
    for layer_index in range(LAYERS):
        normed = layer_norm(stream, norm_gain[layer_index, 0], norm_shift[layer_index, 0]).astype(
            jnp.bfloat16
        )
        projected = jnp.einsum(
            "td,cde->cte", normed, heads_weight[layer_index], preferred_element_type=jnp.float32
        )
        query_rows = (projected[0] + offsets[layer_index, 0]).astype(jnp.bfloat16)
        key_rows = projected[1].astype(jnp.bfloat16)
        value_rows = (projected[2] + offsets[layer_index, 1]).astype(jnp.bfloat16)
        blended, logsum = lax.map(
            lambda record: attend_sequence(record[0], record[1], record[2], record[3]),
            (
                to_heads(query_rows, sequences, local_heads),
                to_heads(key_rows, sequences, local_heads),
                to_heads(value_rows, sequences, local_heads),
                offsets_rows,
            ),
        )
        blended_rows = blended.reshape(row_count, local_width)
        partial_sum = jnp.dot(
            blended_rows, merge_weight[layer_index], preferred_element_type=jnp.float32
        )
        middle = add_branch(stream, partial_sum, branch_bias[layer_index, 0])
        normed_two = layer_norm(
            middle, norm_gain[layer_index, 1], norm_shift[layer_index, 1]
        ).astype(jnp.bfloat16)
        hidden = (
            jnp.dot(normed_two, expand_weight[layer_index], preferred_element_type=jnp.float32)
            + hidden_bias[layer_index]
        )
        active = gelu_tanh(hidden).astype(jnp.bfloat16)
        partial_sum = jnp.dot(
            active, shrink_weight[layer_index], preferred_element_type=jnp.float32
        )
        kept_values.append(
            (
                stream,
                normed,
                query_rows,
                key_rows,
                value_rows,
                logsum,
                blended_rows,
                middle,
                normed_two,
                hidden,
                active,
            )
        )
        stream = add_branch(middle, partial_sum, branch_bias[layer_index, 1])
    output = stream.astype(jnp.bfloat16)
    upstream = cotangent.astype(jnp.float32)
    layer_grads = [None] * LAYERS
    for layer_index in reversed(range(LAYERS)):
        (
            stream_in,
            normed,
            query_rows,
            key_rows,
            value_rows,
            logsum,
            blended_rows,
            middle,
            normed_two,
            hidden,
            active,
        ) = kept_values[layer_index]
        grad_second = upstream.astype(jnp.bfloat16)
        bias_second = jnp.sum(grad_second, axis=0, dtype=jnp.float32)
        shrink_grad = jnp.einsum(
            "tf,td->fd", active, grad_second, preferred_element_type=jnp.float32
        )
        grad_active = jnp.einsum(
            "td,fd->tf", grad_second, shrink_weight[layer_index], preferred_element_type=jnp.float32
        )
        _, gelu_pullback = jax.vjp(gelu_tanh, hidden)
        grad_pre = gelu_pullback(grad_active)[0].astype(jnp.bfloat16)
        hidden_grad = jnp.sum(grad_pre, axis=0, dtype=jnp.float32)
        expand_grad = jnp.einsum(
            "td,tf->df", normed_two, grad_pre, preferred_element_type=jnp.float32
        )
        grad_normed_two = reduce_inputs(
            jnp.einsum(
                "tf,df->td",
                grad_pre,
                expand_weight[layer_index],
                preferred_element_type=jnp.float32,
            )
        )
        _, norm_pullback = jax.vjp(
            layer_norm, middle, norm_gain[layer_index, 1], norm_shift[layer_index, 1]
        )
        grad_middle, gain_second, shift_second = norm_pullback(grad_normed_two)
        grad_middle = grad_middle + upstream
        grad_first = grad_middle.astype(jnp.bfloat16)
        bias_first = jnp.sum(grad_first, axis=0, dtype=jnp.float32)
        merge_grad = jnp.einsum(
            "te,td->ed", blended_rows, grad_first, preferred_element_type=jnp.float32
        )
        grad_blended = jnp.einsum(
            "td,ed->te", grad_first, merge_weight[layer_index], preferred_element_type=jnp.float32
        ).astype(jnp.bfloat16)
        grad_query, grad_keys, grad_values = lax.map(
            lambda record: attend_back(
                record[0], record[1], record[2], record[3], record[4], record[5]
            ),
            (
                to_heads(query_rows, sequences, local_heads),
                to_heads(key_rows, sequences, local_heads),
                to_heads(value_rows, sequences, local_heads),
                offsets_rows,
                logsum,
                to_heads(grad_blended, sequences, local_heads),
            ),
        )
        grad_stack = jnp.stack(
            [
                grad_query.reshape(row_count, local_width),
                grad_keys.reshape(row_count, local_width),
                grad_values.reshape(row_count, local_width),
            ]
        )
        heads_grad = jnp.einsum(
            "td,cte->cde", normed, grad_stack, preferred_element_type=jnp.float32
        )
        offsets_grad = jnp.stack(
            [
                jnp.sum(grad_stack[0], axis=0, dtype=jnp.float32),
                jnp.sum(grad_stack[2], axis=0, dtype=jnp.float32),
            ]
        )
        grad_normed = reduce_inputs(
            jnp.einsum(
                "cte,cde->td",
                grad_stack,
                heads_weight[layer_index],
                preferred_element_type=jnp.float32,
            )
        )
        _, norm_pullback = jax.vjp(
            layer_norm, stream_in, norm_gain[layer_index, 0], norm_shift[layer_index, 0]
        )
        grad_stream, gain_first, shift_first = norm_pullback(grad_normed)
        upstream = grad_stream + grad_middle
        gradients = (
            jnp.stack([gain_first, gain_second]),
            jnp.stack([shift_first, shift_second]),
            heads_grad,
            offsets_grad,
            merge_grad,
            jnp.stack([bias_first, bias_second]),
            expand_grad,
            hidden_grad,
            shrink_grad,
        )
        layer_grads[layer_index] = gradients
    stacked = tuple(
        (
            jnp.stack([layer_grads[layer_index][member] for layer_index in range(LAYERS)])
            for member in range(9)
        )
    )
    stacked = reduce_grads(stacked)
    return (
        output,
        upstream.astype(jnp.bfloat16),
        stacked[0],
        stacked[1],
        stacked[2],
        stacked[3],
        stacked[4],
        stacked[5],
        stacked[6],
        stacked[7],
        stacked[8],
    )


def solution(mesh):
    placed = (
        P("dp", None),
        P("dp"),
        P(),
        P(),
        P(None, None, None, "tensor"),
        P(None, None, "tensor"),
        P(None, "tensor", None),
        P(),
        P(None, None, "tensor"),
        P(None, "tensor"),
        P(None, "tensor", None),
        P("dp", None),
    )
    return jax.shard_map(
        on_device,
        mesh=mesh,
        in_specs=placed,
        out_specs=(
            P("dp", None),
            P("dp", None),
            P(),
            P(),
            P(None, None, None, "tensor"),
            P(None, None, "tensor"),
            P(None, "tensor", None),
            P(),
            P(None, None, "tensor"),
            P(None, "tensor"),
            P(None, "tensor", None),
        ),
        check_vma=False,
    )
```

profile of v0, /device:TPU:0, one launch (start us, length us, event | category | flops | bytes accessed | tf_op | source)
XLA Modules:
  0.0 1735.9 jit_solution(12662325267341914894)
XLA Ops:
  22.9 25.3 %while.94 = (s32[]{:T(128)}, bf16[2,512,6,64]{1,3,2,0:T(8,128)(2,1)S(1)}, f32[2,6,512]{2,1,0:T(8,128)S(1)}, s32[2]{0:T(128)S(1)}, s32[2,512]{1,0:T(2,128)S(1)}, ...) while((s32[]{:T(128)}, ...), condition=%wide.region_5.6_spmd, body=%wide.region_2.5_spmd.sunk | while | flops 844822528 | bytes 42338456 | solution.py:56
  54.6 24.6 %all-reduce.27.cloned.1.call-done = f32[1024,768]{1,0:T(8,128)} async-done(((f32[1024,768]{1,0:T(8,128)}), f32[1024,768]{1,0:T(8,128)}) %all-reduce.27.cloned.1.call-update) | async-done | bytes 3145744 | tf_op jit(solution)/shard_map/psum | solution.py:126
  88.4 5.6 fusion.117
  94.8 23.8 %all-reduce.29.cloned.1.call-done = f32[1024,768]{1,0:T(8,128)} async-done(((f32[1024,768]{1,0:T(8,128)}), f32[1024,768]{1,0:T(8,128)}) %all-reduce.29.cloned.1.call-update) | async-done | bytes 3145744 | tf_op jit(solution)/shard_map/psum | solution.py:126
  130.8 25.1 %while.95 = (s32[]{:T(128)}, bf16[2,512,6,64]{1,3,2,0:T(8,128)(2,1)S(1)}, f32[2,6,512]{2,1,0:T(8,128)S(1)}, s32[2]{0:T(128)S(1)}, s32[2,512]{1,0:T(2,128)S(1)}, ...) while((s32[]{:T(128)}, ...), condition=%wide.region_15.16_spmd, body=%wide.region_12.15_spmd.sunk | while | flops 844822528 | bytes 42338456 | solution.py:56
  159.9 24.5 %all-reduce.31.cloned.1.call-done = f32[1024,768]{1,0:T(8,128)} async-done(((f32[1024,768]{1,0:T(8,128)}), f32[1024,768]{1,0:T(8,128)}) %all-reduce.31.cloned.1.call-update) | async-done | bytes 3145744 | tf_op jit(solution)/shard_map/psum | solution.py:126
  193.3 9.4 convert_reduce_fusion
  208.8 24.5 %all-reduce.33.cloned.1.call-done = f32[1024,768]{1,0:T(8,128)} async-done(((f32[1024,768]{1,0:T(8,128)}), f32[1024,768]{1,0:T(8,128)}) %all-reduce.33.cloned.1.call-update) | async-done | bytes 3145744 | tf_op jit(solution)/shard_map/psum | solution.py:130
  250.1 56.3 %while.96 = (s32[]{:T(128)}, f32[1024,6,64]{0,2,1:T(8,128)}, f32[1024,6,64]{0,2,1:T(8,128)}, bf16[2,512,6,64]{1,3,2,0:T(8,128)(2,1)}, bf16[2,512,6,64]{1,3,2,0:T...) while((s32[]{:T(128)}, f32[1024,6,64]{0,2,1:T(8,128)}, ...), condition=%wide.region_25.26_spmd.clone, body=%wide.region_23.25_spmd.clone.sunk | while | flops 2064381952 | bytes 141793600 | solution.py:107
  258.2 5.4 multiply_reduce_fusion.13
  263.6 5.1 multiply_convert_fusion.10
  268.7 5.7 fusion.271
  280.7 5.2 bitcast_add_fusion.9
  285.9 5.4 multiply_reduce_fusion.13
  291.3 5.1 multiply_convert_fusion.10
  296.4 5.7 fusion.271
  313.9 5.4 convolution_bitcast_fusion.9
  321.2 6.6 convolution_bitcast_fusion.2
  327.9 9.4 convolution_bitcast_fusion
  337.3 6.6 all-reduce.35.cloned.1.call-done
  352.0 8.4 convert_reduce_fusion.1
  367.1 6.0 convolution_bitcast_fusion.6
  375.9 6.5 convolution_bitcast_fusion.1
  382.4 4.5 pad_maximum_fusion.1
  387.0 11.6 reshape.643
  398.7 4.9 convolution_bitcast_fusion.3
  403.6 6.9 pad_maximum_fusion
  410.5 10.5 reshape.639
  439.4 56.3 %while.97 = (s32[]{:T(128)}, f32[1024,6,64]{0,2,1:T(8,128)}, f32[1024,6,64]{0,2,1:T(8,128)}, bf16[2,512,6,64]{1,3,2,0:T(8,128)(2,1)}, bf16[2,512,6,64]{1,3,2,0:T...) while((s32[]{:T(128)}, f32[1024,6,64]{0,2,1:T(8,128)}, ...), condition=%wide.region_34.35_spmd.clone, body=%wide.region_32.34_spmd.clone.sunk | while | flops 2064381952 | bytes 138647840 | solution.py:107
  447.8 5.4 multiply_reduce_fusion.14
  453.2 5.1 multiply_convert_fusion.11
  458.3 5.7 fusion.283
  470.3 5.2 bitcast_add_fusion.11
  475.5 5.4 multiply_reduce_fusion.14
  480.9 5.1 multiply_convert_fusion.11
  486.0 5.7 fusion.283
  511.6 8.0 copy.84
  519.6 8.2 reshape.631
  528.5 9.2 fusion.107
  543.6 720.4 %all-reduce.39.cloned.1.call-done = (f32[1769472]{0:T(1024)}, f32[589824]{0:T(1024)}, f32[2359296]{0:T(1024)}, f32[2359296]{0:T(1024)}) async-done(((f32[1769472]{0:T(1024)}, f32[589824]{0:T(1024)}, f32[2359296]{0:T(1024)}, f32[2359296]{0:T(1024)}), (f32[1769472]{0:T(1024)}, f32[589824]{0:T(1024)}, f32[2359296]{0:T(1024)}, f32[2359296]{0:T(1024)})) %all-reduce.39.cloned.1.call-update) | async-done | bytes 28311568
  1276.8 21.7 %all-reduce.41.cloned.1.call-done = (f32[1024,768]{1,0:T(8,128)}, f32[1024,768]{1,0:T(8,128)}) async-done(((f32[1024,768]{1,0:T(8,128)}, f32[1024,768]{1,0:T(8,128)}), (f32[1024,768]{1,0:T(8,128)}, f32[1024,768]{1,0:T(8,128)})) %all-reduce.41.cloned.1.call-update) | async-done | bytes 6291472 | tf_op jit(solution)/shard_map/psum | solution.py:126
  1304.9 77.8 %all-reduce.15 = (f32[3072]{0:T(1024)S(1)}, f32[3072]{0:T(1024)S(1)}, f32[1536]{0:T(1024)S(1)}, f32[3072]{0:T(1024)S(1)}, f32[3072]{0:T(1024)S(1)}) all-reduce(f32[3072]{0:T(1024)S(1)} %reshape.623, f32[3072]{0:T(1024)S(1)} %reshape.629, f32[1536]{0:T(1024)S(1)} %reshape.633, ...), channel_id=2, replica_groups=mesh['dp'=16,'tensor'=2] {'dp'}, use_global_device_ids=true, to_apply=%region_42.43.clone | all-reduce | flops 13824 | bytes 110592
  1383.5 73.6 %all-reduce.14 = (f32[3072]{0:T(1024)S(1)}, f32[3072]{0:T(1024)S(1)}, f32[1536]{0:T(1024)S(1)}, f32[3072]{0:T(1024)S(1)}, f32[3072]{0:T(1024)S(1)}) all-reduce(f32[3072]{0:T(1024)S(1)} %dynamic-slice_dynamic-update-slice_fusion.3, f32[3072]{0:T(1024)S(1)} %dynamic-slice_dynamic-update-slice_fusion.2, ...), channel_id=1, replica_groups=mesh['dp'=16,'tensor'=2] {'dp'}, use_global_device_ids=true, to_apply=%add | all-reduce | flops 13824 | bytes 110592
  1472.0 8.8 reshape.632
  1480.8 113.2 %all-gather.11.cloned.1.call-done = f32[2359296]{0:T(1024)} async-done(((f32[147456]{0:T(1024)}), f32[2359296]{0:T(1024)}) %all-gather.11.cloned.1.call-update) | async-done | bytes 9437200 | tf_op jit(solution)/shard_map/all_gather | solution.py:136
  1594.1 11.3 reshape.644
  1605.4 112.6 %all-gather.9.cloned.1.call-done = f32[2359296]{0:T(1024)} async-done(((f32[147456]{0:T(1024)}), f32[2359296]{0:T(1024)}) %all-gather.9.cloned.1.call-update) | async-done | bytes 9437200 | tf_op jit(solution)/shard_map/all_gather | solution.py:136
  1718.0 10.9 reshape.640
  (593 shorter events, 256.5 us)
Async XLA Ops:
  7.2 71.9 %all-reduce.27.cloned.1.call-start = ((), (), s32[]{:S(2)}) async-start(), calls=%async_computation | async-start | bytes 6291456 | tf_op jit(solution)/shard_map/psum | solution.py:126
  11.8 70.9 %copy-start.73 = (f32[768]{0:T(1024)}, f32[768]{0:T(1024)S(1)}, u32[]{:S(2)}) copy-start(f32[768]{0:T(1024)S(1)} %get-tuple-element.639) | copy-start | bytes 9220
  11.8 70.9 %copy-start.126 = (f32[768]{0:T(1024)}, f32[768]{0:T(1024)S(1)}, u32[]{:S(2)}) copy-start(f32[768]{0:T(1024)S(1)} %get-tuple-element.489) | copy-start | bytes 9220
  53.1 65.5 %all-reduce.29.cloned.1.call-start = ((), (), s32[]{:S(2)}) async-start(), calls=%async_computation.1 | async-start | bytes 6291456 | tf_op jit(solution)/shard_map/psum | solution.py:126
  54.6 31.1 %copy-start.117 = (f32[1536]{0:T(1024)}, f32[1536]{0:T(1024)S(1)}, u32[]{:S(2)}) copy-start(f32[1536]{0:T(1024)S(1)} %get-tuple-element.483) | copy-start | bytes 18436
  82.1 36.4 %copy-start.8 = (f32[1024,768]{1,0:T(8,128)}, f32[1024,768]{1,0:T(8,128)S(1)}, u32[]{:S(2)}) copy-start(f32[1024,768]{1,0:T(8,128)S(1)} %get-tuple-element.609) | copy-start | bytes 9437188
  94.0 90.4 %all-reduce.31.cloned.1.call-start = ((), (), s32[]{:S(2)}) async-start(), calls=%async_computation.2 | async-start | bytes 6291456 | tf_op jit(solution)/shard_map/psum | solution.py:126
  157.1 27.3 %copy-start.98 = (f32[768]{0:T(1024)S(1)}, f32[768]{0:T(1024)}, u32[]{:S(2)}) copy-start(f32[768]{0:T(1024)} %get-tuple-element.481) | copy-start | bytes 9220
  159.9 73.4 %all-reduce.33.cloned.1.call-start = ((), (), s32[]{:S(2)}) async-start(), calls=%async_computation.3 | async-start | bytes 6291456 | tf_op jit(solution)/shard_map/psum | solution.py:130
  187.8 49.9 %copy-start.71 = (f32[1024]{0:T(1024)}, f32[1024]{0:T(1024)S(1)}, u32[]{:S(2)}) copy-start(f32[1024]{0:T(1024)S(1)} %broadcast_multiply_fusion) | copy-start | bytes 12292
  188.4 49.4 %copy-start.87 = (f32[1024]{0:T(1024)}, f32[1024]{0:T(1024)S(1)}, u32[]{:S(2)}) copy-start(f32[1024]{0:T(1024)S(1)} %fusion.162) | copy-start | bytes 12292
  208.7 135.2 %all-reduce.35.cloned.1.call-start = ((), (), s32[]{:S(2)}) async-start(), calls=%async_computation.4 | async-start | bytes 6291456 | tf_op jit(solution)/shard_map/psum | solution.py:130
  319.4 101.7 %all-reduce.37.cloned.1.call-start = ((), (), s32[]{:S(2)}) async-start(), calls=%async_computation.5 | async-start | bytes 6291456 | tf_op jit(solution)/shard_map/psum | solution.py:130
  327.8 16.1 copy-start.11
  327.8 16.1 copy-start.70
  327.8 16.1 copy-start.76
  327.8 16.1 copy-start.86
  337.3 10.3 copy-start.96
  349.9 12.2 slice-start.6
  352.0 10.1 slice-start.7
  366.4 897.6 %all-reduce.39.cloned.1.call-start = ((), (), s32[]{:S(2)}) async-start(), calls=%async_computation.10 | async-start | bytes 56623104
  387.0 11.7 copy-start.9
  387.0 11.7 copy-start.68
  387.0 11.7 copy-start.74
  387.0 11.7 copy-start.84
  387.0 11.7 copy-start.127
  527.9 770.7 %all-reduce.41.cloned.1.call-start = ((), (), s32[]{:S(2)}) async-start(), calls=%async_computation.11 | async-start | bytes 12582912 | tf_op jit(solution)/shard_map/psum | solution.py:126
  541.8 733.9 %copy-start.121 = (f32[1536]{0:T(1024)S(1)}, f32[1536]{0:T(1024)}, u32[]{:S(2)}) copy-start(f32[1536]{0:T(1024)} %get-tuple-element.633) | copy-start | bytes 18436
  541.8 733.9 %copy-start.100 = (f32[768]{0:T(1024)S(1)}, f32[768]{0:T(1024)}, u32[]{:S(2)}) copy-start(f32[768]{0:T(1024)} %get-tuple-element.469) | copy-start | bytes 9220
  541.8 733.9 %copy-start.99 = (f32[768]{0:T(1024)S(1)}, f32[768]{0:T(1024)}, u32[]{:S(2)}) copy-start(f32[768]{0:T(1024)} %get-tuple-element.477) | copy-start | bytes 9220
  541.8 733.9 %copy-start.101 = (f32[768]{0:T(1024)S(1)}, f32[768]{0:T(1024)}, u32[]{:S(2)}) copy-start(f32[768]{0:T(1024)} %get-tuple-element.592) | copy-start | bytes 9220
  541.8 734.0 %copy-start.36 = (bf16[2,512,6,64]{1,3,2,0:T(8,128)(2,1)S(1)}, bf16[2,512,6,64]{1,3,2,0:T(8,128)(2,1)}, u32[]{:S(2)}) copy-start(bf16[2,512,6,64]{1,3,2,0:T(8,128)(2,1)} %get-tuple-element.321) | copy-start | bytes 2359300
  541.8 734.2 %copy-start.109 = (f32[6,64]{1,0:T(8,128)S(1)}, f32[6,64]{1,0:T(8,128)}, u32[]{:S(2)}) copy-start(f32[6,64]{1,0:T(8,128)} %get-tuple-element.596) | copy-start | bytes 4612
  541.8 734.3 %copy-start.103 = (f32[768]{0:T(1024)S(1)}, f32[768]{0:T(1024)}, u32[]{:S(2)}) copy-start(f32[768]{0:T(1024)} %get-tuple-element.467) | copy-start | bytes 9220
  541.8 734.3 %copy-start.105 = (f32[768]{0:T(1024)S(1)}, f32[768]{0:T(1024)}, u32[]{:S(2)}) copy-start(f32[768]{0:T(1024)} %get-tuple-element.590) | copy-start | bytes 9220
  541.9 734.3 %copy-start.104 = (f32[768]{0:T(1024)S(1)}, f32[768]{0:T(1024)}, u32[]{:S(2)}) copy-start(f32[768]{0:T(1024)} %get-tuple-element.630) | copy-start | bytes 9220
  541.9 734.3 %copy-start.102 = (f32[768]{0:T(1024)S(1)}, f32[768]{0:T(1024)}, u32[]{:S(2)}) copy-start(f32[768]{0:T(1024)} %get-tuple-element.476) | copy-start | bytes 9220
  541.9 734.3 %copy-start.122 = (f32[1536]{0:T(1024)S(1)}, f32[1536]{0:T(1024)}, u32[]{:S(2)}) copy-start(f32[1536]{0:T(1024)} %get-tuple-element.635) | copy-start | bytes 18436
  541.9 926.8 %all-gather.7.cloned.1.call-start = ((), (), s32[]{:S(2)}) async-start(), calls=%async_computation.7 | async-start | bytes 2506752 | tf_op jit(solution)/shard_map/all_gather | solution.py:136
  1264.1 12.3 copy-start.107
  1264.1 12.3 copy-start.106
  1264.1 12.3 copy-start.108
  1265.7 206.3 %all-gather.5.cloned.1.call-start = ((), (), s32[]{:S(2)}) async-start(), calls=%async_computation.6 | async-start | bytes 7520256 | tf_op jit(solution)/shard_map/all_gather | solution.py:136
  1268.2 325.8 %all-gather.11.cloned.1.call-start = ((), (), s32[]{:S(2)}) async-start(), calls=%async_computation.9 | async-start | bytes 10027008 | tf_op jit(solution)/shard_map/all_gather | solution.py:136
  1270.9 447.1 %all-gather.9.cloned.1.call-start = ((), (), s32[]{:S(2)}) async-start(), calls=%async_computation.8 | async-start | bytes 10027008 | tf_op jit(solution)/shard_map/all_gather | solution.py:136
  1275.8 25.7 %copy-start.92 = (f32[1024]{0:T(1024)S(1)}, f32[1024]{0:T(1024)}, u32[]{:S(2)}) copy-start(f32[1024]{0:T(1024)} %copy-done.91) | copy-start | bytes 12292
  1301.3 158.8 %copy-start.7 = (f32[1024,768]{1,0:T(8,128)S(1)}, f32[1024,768]{1,0:T(8,128)}, u32[]{:S(2)}) copy-start(f32[1024,768]{1,0:T(8,128)} %copy-done.4) | copy-start | bytes 9437188
  1301.3 158.8 %copy-start.97 = (f32[768]{0:T(1024)S(1)}, f32[768]{0:T(1024)}, u32[]{:S(2)}) copy-start(f32[768]{0:T(1024)} %get-tuple-element.478) | copy-start | bytes 9220
  (127 other events, 469.8 us)
Sparse Core Ops, SparseCore 0:
  53.2 25.8 all-reduce.26
  94.1 24.4 all-reduce.28
  160.0 24.3 all-reduce.30
  208.8 24.3 all-reduce.32
  319.5 24.3 all-reduce.34
  366.6 24.3 all-reduce.36
  528.0 736.0 all-reduce.38
  1267.4 31.1 all-reduce.40
  1301.9 64.4 all-gather.6
  1369.7 100.7 all-gather.4
  1473.2 120.7 all-gather.10
  1597.3 120.6 all-gather.8
where the time goes:
time: 1740 us
  waiting for transfers between devices  1070 us (61%)
  matrix products  222 us (13%)
  blocking collectives  151 us (9%)
  local copies, waits for them, and re-layouts  144 us (8%)
  other arithmetic  116 us (7%)
  between operations  21 us (1%)
    unnamed x13, waiting for transfers between devices  721 us
    all_gather x4, waiting for transfers between devices, reduce_grads(): summed = lax.all_gather(shares, 'dp', axis=0, tiled=True)  226 us
    unnamed x2, blocking collectives  151 us
    psum x4, waiting for transfers between devices, add_branch(): return stream + (lax.psum(partial_sum, 'tensor') + bias_row)  94.5 us
    reshape x9, local copies, waits for them, and re-layouts, reduce_grads(): whole.reshape(member.shape)  37.4 us
  transfers between devices with their start and end apart: 12, of which 9 were waited for; matrix products, arithmetic and copies ran while one was open for 8% of the time, Pallas kernels for 0%

commit v1 on v0

--- a/solution.py
+++ b/solution.py
@@ -1,11 +1,333 @@
 import jax
 import jax.numpy as jnp
 from jax import lax
+from jax.experimental import pallas as pl
+from jax.experimental.pallas import tpu as pltpu
 from jax.sharding import PartitionSpec as P
+MESH = pl.DeviceIdType.MESH
+
+
+class Exchange:
+    def __init__(self, groups, rows, cols, slots, lags):
+        self.groups, self.rows, self.cols, self.slots = groups, rows, cols, slots
+        self.half = rows // 2
+        self.chunk = self.half // 4
+        starts = [0]
+        for lag in lags:
+            starts.append(starts[-1] + lag)
+        self.starts = starts
+        self.ticks = groups + starts[-1]
+        self.last_slots = starts[9]
+        self.gather_slots = max(starts[8] - starts[1], slots)
+
+    def scratch(self):
+        groups, slots, half, chunk, cols = self.groups, self.slots, self.half, self.chunk, self.cols
+        dma = pltpu.SemaphoreType.DMA
+        plain = pltpu.SemaphoreType.REGULAR
+        return dict(
+            held=pltpu.VMEM((self.held_slots(), 2, half, cols), jnp.float32),
+            swap_in=pltpu.VMEM((slots, 2, half, cols), jnp.float32),
+            chain_in=pltpu.VMEM((slots, 3, 2, 2, chunk, cols), jnp.float32),
+            third_in=pltpu.VMEM((slots, 2, chunk, cols), jnp.float32),
+            swap_s=dma((slots,)), swap_r=dma((slots,)),
+            chain_s=dma((slots, 3, 2)), chain_r=dma((slots, 3, 2)),
+            third_s=dma((slots,)), third_r=dma((slots,)),
+            gather_s=dma((slots, 3, 2)), gather_r=dma((self.gather_slots, 3, 2)),
+            last_s=dma((slots,)), last_r=dma((self.last_slots,)),
+            own_s=dma((slots,)), load_s=dma((slots,)),
+            swap_c=plain((2,)), chain_c=plain((3, 2)), third_c=plain((2,)),
+        )
+
+    def held_slots(self):
+        return self.groups
+
+    def setup(self, refs):
+        self.refs = refs
+        dp = lax.axis_index("dp")
+        core = lax.axis_index("tensor")
+        low = lax.rem(dp, 16)
+        self.dp, self.core = dp, core
+        self.z = lax.div(low, 4)
+        self.y = lax.rem(lax.div(low, 2), 2)
+        self.x = lax.rem(low, 2)
+        self.step_x = 1 - 2 * self.x
+        self.step_y = 2 - 4 * self.y
+        self.along = ((dp + 4, core), (dp - 4, core))
+
+    def barrier(self, others=()):
+        z = self.z
+        bar = pltpu.get_barrier_semaphore()
+
+        def greet(device):
+            pl.semaphore_signal(bar, inc=1, device_id=device, device_id_type=MESH)
+
+        for device in ((self.dp + self.step_x, self.core), (self.dp + self.step_y, self.core)) + tuple(others):
+            greet(device)
+
+        @pl.when(z < 3)
+        def _():
+            greet(self.along[0])
+
+        @pl.when(z > 0)
+        def _():
+            greet(self.along[1])
+
+        pl.semaphore_wait(bar, 2 + len(others) + (z < 3).astype(jnp.int32) + (z > 0).astype(jnp.int32))
+
+    def first(self, g):
+        return (self.dp + jnp.where(lax.rem(g, 2) == 0, self.step_x, self.step_y), self.core)
+
+    def third(self, g):
+        return (self.dp + jnp.where(lax.rem(g, 2) == 0, self.step_y, self.step_x), self.core)
+
+    def side(self, g):
+        return jnp.where(lax.rem(g, 2) == 0, self.x, self.y)
+
+    def copy(self, src, dst, send, recv, device):
+        return pltpu.make_async_remote_copy(
+            src_ref=src, dst_ref=dst, send_sem=send, recv_sem=recv, device_id=device, device_id_type=MESH
+        )
+
+    def rows_of(self, j):
+        return pl.ds(pl.multiple_of(j * self.chunk, 8), self.chunk)
+
+    def held(self, g):
+        return self.refs["held"].at[g]
+
+    def swap(self, g):
+        r, k = self.refs, lax.rem(g, self.slots)
+        return self.copy(self.sent_half(g), r["swap_in"].at[k], r["swap_s"].at[k], r["swap_r"].at[k], self.first(g))
+
+    def chain_send(self, step, d, g):
+        z, r, k = self.z, self.refs, lax.rem(g, self.slots)
+        j = 4 - step + z if d == 0 else step - 4 + z
+        here = ((z < 3) & (step > z)) if d == 0 else ((z > 0) & (step > 3 - z))
+        at = (k, step - 1, d)
+        part = self.held(g).at[:, self.rows_of(j)]
+        return here, self.copy(part, r["chain_in"].at[at], r["chain_s"].at[at], r["chain_r"].at[at], self.along[d])
+
+    def start_chain(self, step, g):
+        for d in range(2):
+            here, copy = self.chain_send(step, d, g)
+
+            @pl.when(here)
+            def _():
+                @pl.when(g >= self.slots)
+                def _():
+                    pl.semaphore_wait(self.refs["chain_c"].at[step - 1, d], 1)
+
+                copy.start()
+
+    def finish_chain(self, step, g):
+        z, r, k = self.z, self.refs, lax.rem(g, self.slots)
+        for d in range(2):
+            here, copy = self.chain_send(step, d, g)
+
+            @pl.when(here)
+            def _():
+                copy.wait_send()
+
+        for d in range(2):
+            here = ((z >= 1) & (step >= z)) if d == 0 else ((z <= 2) & (step >= 3 - z))
+            j = 3 - step + z if d == 0 else step - 3 + z
+            at = (k, step - 1, d)
+
+            @pl.when(here)
+            def _():
+                came = r["chain_in"].at[at]
+                self.copy(came, came, r["chain_s"].at[at], r["chain_r"].at[at], self.along[1 - d]).wait_recv()
+                part = self.held(g).at[:, self.rows_of(j)]
+                part[...] = part[...] + came[...]
+
+                @pl.when(g + self.slots < self.groups)
+                def _():
+                    pl.semaphore_signal(
+                        r["chain_c"].at[step - 1, d], inc=1, device_id=self.along[1 - d], device_id_type=MESH
+                    )
+
+    def third_swap(self, g):
+        r, k = self.refs, lax.rem(g, self.slots)
+        part = self.held(g).at[:, self.rows_of(self.z)]
+        return self.copy(part, r["third_in"].at[k], r["third_s"].at[k], r["third_r"].at[k], self.third(g))
+
+    def gather_copy(self, step, d, g, j, source=None):
+        r, k = self.refs, lax.rem(g, self.slots)
+        part = self.result(g, self.side(g) * self.half + j * self.chunk, self.chunk)
+        return self.copy(
+            part if source is None else source,
+            part,
+            r["gather_s"].at[k, step - 1, d],
+            r["gather_r"].at[lax.rem(g, self.gather_slots), step - 1, d],
+            self.along[d],
+        )
+
+    def gather_send(self, step, d, g):
+        z = self.z
+        j = z - (step - 1) if d == 0 else z + step - 1
+        here = ((z < 3) & (step - 1 <= z)) if d == 0 else ((z > 0) & (z + step - 1 <= 3))
+        source = self.held(g).at[:, self.rows_of(z)] if step == 1 else None
+        return here, self.gather_copy(step, d, g, j, source)
+
+    def start_gather(self, step, g):
+        for d in range(2):
+            here, copy = self.gather_send(step, d, g)
+
+            @pl.when(here)
+            def _():
+                copy.start()
+
+    def finish_gather(self, step, g):
+        z = self.z
+        for d in range(2):
+            here, copy = self.gather_send(step, d, g)
+
+            @pl.when(here)
+            def _():
+                copy.wait_send()
+
+        for d in range(2):
+            here = (z >= step) if d == 0 else (z + step <= 3)
+            j = z - step if d == 0 else z + step
+
+            @pl.when(here)
+            def _():
+                self.gather_copy(step, d, g, j).wait_recv()
+
+    def own_copy(self, g):
+        k = lax.rem(g, self.slots)
+        part = self.held(g).at[:, self.rows_of(self.z)]
+        return pltpu.make_async_copy(
+            part, self.result(g, self.side(g) * self.half + self.z * self.chunk, self.chunk), self.refs["own_s"].at[k]
+        )
+
+    def last(self, g):
+        r, k = self.refs, lax.rem(g, self.slots)
+        part = self.result(g, self.side(g) * self.half, self.half)
+        return self.copy(part, part, r["last_s"].at[k], r["last_r"].at[lax.rem(g, self.last_slots)], self.first(g))
+
+    def stage(self, e, g):
+        r, slots, groups = self.refs, self.slots, self.groups
+        k = lax.rem(g, slots)
+        if e == 0:
+            self.prepare(g)
+
+            @pl.when(g >= slots)
+            def _():
+                pl.semaphore_wait(r["swap_c"].at[lax.rem(g, 2)], 1)
+
+            self.swap(g).start()
+        elif e == 1:
+            self.settle(g)
+            copy = self.swap(g)
+            copy.wait_send()
+            copy.wait_recv()
+            mine = self.held(g)
+            mine[...] = mine[...] + r["swap_in"][k]
+
+            @pl.when(g + slots < groups)
+            def _():
+                pl.semaphore_signal(
+                    r["swap_c"].at[lax.rem(g, 2)], inc=1, device_id=self.first(g), device_id_type=MESH
+                )
+
+            self.start_chain(1, g)
+        elif e in (2, 3):
+            self.finish_chain(e - 1, g)
+            self.start_chain(e, g)
+        elif e == 4:
+            self.finish_chain(3, g)
+
+            @pl.when(g >= slots)
+            def _():
+                pl.semaphore_wait(r["third_c"].at[lax.rem(g, 2)], 1)
+
+            self.third_swap(g).start()
+        elif e == 5:
+            copy = self.third_swap(g)
+            copy.wait_send()
+            copy.wait_recv()
+            part = self.held(g).at[:, self.rows_of(self.z)]
+            part[...] = part[...] + r["third_in"][k]
+
+            @pl.when(g + slots < groups)
+            def _():
+                pl.semaphore_signal(
+                    r["third_c"].at[lax.rem(g, 2)], inc=1, device_id=self.third(g), device_id_type=MESH
+                )
+
+            self.start_gather(1, g)
+            self.own_copy(g).start()
+        elif e in (6, 7):
+            self.finish_gather(e - 5, g)
+            self.start_gather(e - 4, g)
+        elif e == 8:
+            self.finish_gather(3, g)
+            self.own_copy(g).wait()
+            self.last(g).start()
+        else:
+            copy = self.last(g)
+            copy.wait_send()
+            copy.wait_recv()
+
+    def tick(self, t):
+        for e in reversed(range(10)):
+            g = t - self.starts[e]
+
+            @pl.when((g >= 0) & (g < self.groups))
+            def _():
+                self.stage(e, g)
+
+
+class FlatExchange(Exchange):
+    def sent_half(self, g):
+        return self.source.at[g, :, pl.ds(pl.multiple_of((1 - self.side(g)) * self.half, 8), self.half)]
+
+    def load(self, g):
+        k = lax.rem(g, self.slots)
+        own = self.source.at[g, :, pl.ds(pl.multiple_of(self.side(g) * self.half, 8), self.half)]
+        return pltpu.make_async_copy(own, self.held(g), self.refs["load_s"].at[k])
+
+    def prepare(self, g):
+        self.load(g).start()
+
+    def settle(self, g):
+        self.load(g).wait()
+
+    def result(self, g, start, size):
+        return self.target.at[g, :, pl.ds(pl.multiple_of(start, 8), size)]
+
+
+def all_reduce(flat, slots=4, lags=(2, 1, 1, 1, 1, 1, 1, 1, 2)):
+    groups, _, rows, cols = flat.shape
+    plan = FlatExchange(groups, rows, cols, slots, lags)
+    scratch = plan.scratch()
+    names = list(scratch)
+
+    def kernel(source, target, *refs):
+        plan.source, plan.target = source, target
+        plan.setup(dict(zip(names, refs)))
+        plan.barrier()
+
+        def step(t, carry):
+            plan.tick(t)
+            return carry
+
+        lax.fori_loop(0, plan.ticks, step, 0)
+
+    return pl.pallas_call(
+        kernel,
+        out_shape=jax.ShapeDtypeStruct(flat.shape, jnp.float32),
+        in_specs=[pl.BlockSpec(memory_space=pl.ANY)],
+        out_specs=pl.BlockSpec(memory_space=pl.ANY),
+        scratch_shapes=[scratch[n] for n in names],
+        compiler_params=pltpu.CompilerParams(collective_id=0, has_side_effects=True, vmem_limit_bytes=60 * 2**20),
+    )(flat)
+
 
 HEAD_DIM = 64
 LEN = 1024
 LAYERS = 2
+UNIT = 384
 
 
 def layer_norm(stream, gain_row, shift_row):
@@ -130,11 +452,63 @@
     return lax.psum(partial_sum, "tensor")
 
 
-def reduce_grads(gradients):
-    flattened = tuple((member.reshape(-1) for member in gradients))
-    shares = lax.psum_scatter(flattened, "dp", scatter_dimension=0, tiled=True)
-    summed = lax.all_gather(shares, "dp", axis=0, tiled=True)
-    return tuple((whole.reshape(member.shape) for whole, member in zip(summed, gradients)))
+BLOCK = 16
+
+
+def columns_to_units(matrix):
+    rows, width = matrix.shape
+    return matrix.reshape(rows, width // UNIT, UNIT).transpose(1, 0, 2)
+
+
+def units_to_columns(units):
+    count, rows, width = units.shape
+    return units.transpose(1, 0, 2).reshape(rows, count * width)
+
+
+def reduce_grads(layers):
+    ranks = lax.axis_size("dp")
+    small = jnp.stack([jnp.concatenate([layer[m].reshape(-1) for m in (0, 1, 3, 5, 7)]) for layer in layers])
+    pieces = []
+    for layer in reversed(layers):
+        heads, merge, expand, shrink = layer[2], layer[4], layer[6], layer[8]
+        depth = expand.shape[0]
+        pieces.append(columns_to_units(shrink).reshape(shrink.shape[1] // UNIT, -1, UNIT, UNIT).transpose(1, 0, 2, 3).reshape(-1, UNIT, UNIT))
+        pieces.append(columns_to_units(expand).reshape(-1, UNIT, UNIT))
+        pieces.append(columns_to_units(merge))
+        pieces.append(heads.reshape(-1, UNIT, UNIT))
+    flat = jnp.concatenate(pieces)
+    flat = flat.reshape(flat.shape[0] // 2, 2, UNIT, UNIT)
+    if ranks % BLOCK:
+        flat = lax.psum(flat, "dp")
+    else:
+        flat = all_reduce(flat)
+        if ranks > BLOCK:
+            groups = [[j * BLOCK + i for j in range(ranks // BLOCK)] for i in range(BLOCK)]
+            flat = lax.psum(flat, "dp", axis_index_groups=groups)
+    small = lax.psum(small, "dp")
+    flat = flat.reshape(-1, UNIT, UNIT)
+    out = []
+    at = 0
+    for layer in reversed(layers):
+        heads, merge, expand, shrink = layer[2], layer[4], layer[6], layer[8]
+        def take(like):
+            nonlocal at
+            n = like.size // (UNIT * UNIT)
+            at += n
+            return flat[at - n : at]
+        shrink_sum = take(shrink).reshape(-1, shrink.shape[1] // UNIT, UNIT, UNIT).transpose(0, 2, 1, 3).reshape(shrink.shape)
+        expand_sum = units_to_columns(take(expand).reshape(-1, expand.shape[0], UNIT))
+        merge_sum = units_to_columns(take(merge))
+        heads_sum = take(heads).reshape(heads.shape)
+        out.append((heads_sum, merge_sum, expand_sum, shrink_sum))
+    out = [jnp.stack(group) for group in zip(*reversed(out))]
+    smalls = []
+    at = 0
+    for m in (0, 1, 3, 5, 7):
+        like = layers[0][m]
+        smalls.append(small[:, at : at + like.size].reshape((len(layers),) + like.shape))
+        at += like.size
+    return (smalls[0], smalls[1], out[0], smalls[2], out[1], smalls[3], out[2], smalls[4], out[3])
 
 
 def to_heads(matrix, sequences, local_heads):
@@ -319,13 +693,7 @@
             shrink_grad,
         )
         layer_grads[layer_index] = gradients
-    stacked = tuple(
-        (
-            jnp.stack([layer_grads[layer_index][member] for layer_index in range(LAYERS)])
-            for member in range(9)
-        )
-    )
-    stacked = reduce_grads(stacked)
+    stacked = reduce_grads(layer_grads)
     return (
         output,
         upstream.astype(jnp.bfloat16),

time: 1740 us -> 1160 us (0.67)
  waiting for transfers between devices: 1070 us -> 97 us
  Pallas kernels: 0 us -> 378 us
  local copies, waits for them, and re-layouts: 144 us -> 220 us
  blocking collectives: 151 us -> 75.1 us
    unnamed x13 -> x7, waiting for transfers between devices: 721 us -> 0.12 us
    pallas_call x0 -> x1, Pallas kernels: none -> 378 us  [all_reduce(): pl.pallas_call(kernel, out_shape=jax.ShapeDtypeStruct(flat.shape, jnp.flo...]
    all_gather x4 -> x0, waiting for transfers between devices: 226 us -> none  [reduce_grads(): summed = lax.all_gather(shares, 'dp', axis=0, tiled=True)]
    unnamed x2 -> x0, blocking collectives: 151 us -> none
    psum x0 -> x1, blocking collectives: none -> 75.1 us  [reduce_grads(): small = lax.psum(small, 'dp')]
    transpose x0 -> x12, local copies, waits for them, and re-layouts: none -> 63.4 us  [the longest x3 26 us: reduce_grads(): take(shrink).reshape(-1, shrink.shape[1] // UNIT, UNIT, UNIT)]
    reshape x18 -> x20, local copies, waits for them, and re-layouts: 71.2 us -> 47.8 us  [the longest x4 27.4 us: reduce_grads(): columns_to_units(shrink).reshape(shrink.shape[1] // UNIT, -1, UNIT, UNIT)]
    psum x4, waiting for transfers between devices: 94.5 us -> 72.4 us  [add_branch(): return stream + (lax.psum(partial_sum, 'tensor') + bias_row)]
  transfers between devices with their start and end apart: 12 -> 7, of which waited for: 9 -> 4; matrix products, arithmetic and copies ran while one was open for 8% -> 21% of each run, Pallas kernels for 0% -> 33%
where the time goes in v1:
time: 1160 us; the launch traced here: 1150 us
  Pallas kernels  378 us (33%)
  matrix products  236 us (20%)
  local copies, waits for them, and re-layouts  220 us (19%)
  other arithmetic  119 us (10%)
  waiting for transfers between devices  97 us (8%)
  blocking collectives  75.1 us (6%)
  between operations  16.5 us (1%)
    pallas_call x1, Pallas kernels, all_reduce(): pl.pallas_call(kernel, out_shape=jax.ShapeDtypeStruct(flat.shape, jnp.flo...  378 us
    psum x1, blocking collectives, reduce_grads(): small = lax.psum(small, 'dp')  75.1 us
    psum x4, waiting for transfers between devices, add_branch(): return stream + (lax.psum(partial_sum, 'tensor') + bias_row)  72.4 us
    unnamed x326, local copies, waits for them, and re-layouts  38.3 us
    reshape x4, local copies, waits for them, and re-layouts, reduce_grads(): columns_to_units(shrink).reshape(shrink.shape[1] // UNIT, -1, UNIT, UNIT)  27.4 us
    another operation x4, local copies, waits for them, and re-layouts, reduce_grads(): out = [jnp.stack(group) for group in zip(*reversed(out))]  27.4 us
    transpose x3, local copies, waits for them, and re-layouts, reduce_grads(): take(shrink).reshape(-1, shrink.shape[1] // UNIT, UNIT, UNIT)  26 us
    psum x3, waiting for transfers between devices, reduce_inputs(): return lax.psum(partial_sum, 'tensor')  24.5 us
  transfers between devices with their start and end apart: 7, of which 4 were waited for; matrix products, arithmetic and copies ran while one was open for 21% of the time, Pallas kernels for 33%

profile of v1, /device:TPU:0, one launch (start us, length us, event | category | flops | bytes accessed | tf_op | source)
XLA Modules:
  0.0 1150.0 jit_solution(17943248318653009610)
XLA Ops:
  22.8 25.1 %while.94 = (s32[]{:T(128)}, bf16[2,512,6,64]{1,3,2,0:T(8,128)(2,1)S(1)}, f32[2,6,512]{2,1,0:T(8,128)S(1)}, s32[2]{0:T(128)S(1)}, s32[2,512]{1,0:T(2,128)S(1)}, ...) while((s32[]{:T(128)}, ...), condition=%wide.region_5.6_spmd, body=%wide.region_2.5_spmd.sunk | while | flops 844822528 | bytes 42338456 | solution.py:378
  54.8 24.2 %all-reduce.9.cloned.1.call-done = f32[1024,768]{1,0:T(8,128)} async-done(((f32[1024,768]{1,0:T(8,128)}), f32[1024,768]{1,0:T(8,128)}) %all-reduce.9.cloned.1.call-update) | async-done | bytes 3145744 | tf_op jit(solution)/shard_map/psum | solution.py:448
  90.3 5.6 fusion.117
  96.7 23.8 %all-reduce.11.cloned.1.call-done = f32[1024,768]{1,0:T(8,128)} async-done(((f32[1024,768]{1,0:T(8,128)}), f32[1024,768]{1,0:T(8,128)}) %all-reduce.11.cloned.1.call-update) | async-done | bytes 3145744 | tf_op jit(solution)/shard_map/psum | solution.py:448
  132.7 25.0 %while.95 = (s32[]{:T(128)}, bf16[2,512,6,64]{1,3,2,0:T(8,128)(2,1)S(1)}, f32[2,6,512]{2,1,0:T(8,128)S(1)}, s32[2]{0:T(128)S(1)}, s32[2,512]{1,0:T(2,128)S(1)}, ...) while((s32[]{:T(128)}, ...), condition=%wide.region_15.16_spmd, body=%wide.region_12.15_spmd.sunk | while | flops 844822528 | bytes 42338456 | solution.py:378
  163.6 24.5 %all-reduce.13.cloned.1.call-done = f32[1024,768]{1,0:T(8,128)} async-done(((f32[1024,768]{1,0:T(8,128)}), f32[1024,768]{1,0:T(8,128)}) %all-reduce.13.cloned.1.call-update) | async-done | bytes 3145744 | tf_op jit(solution)/shard_map/psum | solution.py:448
  197.2 9.2 convert_reduce_fusion
  212.4 24.5 %all-reduce.15.cloned.1.call-done = f32[1024,768]{1,0:T(8,128)} async-done(((f32[1024,768]{1,0:T(8,128)}), f32[1024,768]{1,0:T(8,128)}) %all-reduce.15.cloned.1.call-update) | async-done | bytes 3145744 | tf_op jit(solution)/shard_map/psum | solution.py:452
  252.9 56.4 %while.96 = (s32[]{:T(128)}, f32[1024,6,64]{0,2,1:T(8,128)}, f32[1024,6,64]{0,2,1:T(8,128)}, bf16[2,512,6,64]{1,3,2,0:T(8,128)(2,1)}, bf16[2,512,6,64]{1,3,2,0:T...) while((s32[]{:T(128)}, f32[1024,6,64]{0,2,1:T(8,128)}, ...), condition=%wide.region_25.26_spmd.clone, body=%wide.region_23.25_spmd.clone.sunk | while | flops 2064381952 | bytes 144939360 | solution.py:429
  261.3 5.4 multiply_reduce_fusion.13
  271.8 5.7 fusion.278
  283.8 5.2 bitcast_add_fusion.9
  289.0 5.4 multiply_reduce_fusion.13
  299.5 5.7 fusion.278
  315.3 5.7 convolution_bitcast_fusion.5
  325.1 8.1 fusion.177
  333.2 6.4 reshape.686
  339.6 7.5 copy.67
  347.1 6.5 fusion.176
  353.6 9.3 fusion.107
  370.5 8.4 convert_reduce_fusion.1
  389.8 6.6 reshape.688
  407.3 5.9 convolution_bitcast_fusion.3
  426.6 9.1 fusion.169
  446.8 56.1 %while.97 = (s32[]{:T(128)}, f32[1024,6,64]{0,2,1:T(8,128)}, f32[1024,6,64]{0,2,1:T(8,128)}, bf16[2,512,6,64]{1,3,2,0:T(8,128)(2,1)}, bf16[2,512,6,64]{1,3,2,0:T...) while((s32[]{:T(128)}, f32[1024,6,64]{0,2,1:T(8,128)}, ...), condition=%wide.region_34.35_spmd.clone, body=%wide.region_32.34_spmd.clone.sunk | while | flops 2064381952 | bytes 138647840 | solution.py:429
  454.9 5.4 multiply_reduce_fusion.14
  465.4 5.7 fusion.290
  482.5 5.4 multiply_reduce_fusion.14
  493.0 5.7 fusion.290
  508.9 5.6 convolution_bitcast_fusion.4
  515.4 6.2 reshape.692
  521.6 7.5 copy.72
  529.1 6.7 fusion.175
  535.7 6.5 reshape.694
  554.4 5.8 convolution_bitcast_fusion.2
  570.5 377.7 %shard_map.203 = f32[24,2,384,384]{3,2,1,0:T(8,128)} custom-call(f32[24,2,384,384]{3,2,1,0:T(8,128)} %bitcast.363), custom_call_target="tpu_custom_call" | custom-call | tf_op jit(solution)/shard_map/pallas_call | solution.py:317
  961.6 12.1 %slice_bitcast_fusion.1 = (f32[4,384,2,384]{3,1,2,0:T(8,128)S(1)}, f32[4,384,2,384]{3,1,2,0:T(8,128)}, f32[4,2,384,384]{3,2,1,0:T(8,128)}, f32[4,2,384,384]{3,2,1,0:T(8,128)}) fusion(f32[24,2,384,384]{3,2,1,0:T(8,128)} %shard_map.203), kind=kLoop, calls=%fused_computation.153 | loop fusion | bytes 37748736 | tf_op jit(solution)/shard_map/transpose | solution.py:499
  973.6 5.9 copy.81
  979.5 7.2 stack_reshape.54
  986.7 8.1 copy.82
  994.8 7.3 stack_reshape.55
  1002.1 7.6 copy.80
  1009.6 6.4 stack_reshape.53
  1016.0 7.6 copy.79
  1023.6 6.6 stack_reshape.52
  1042.3 6.9 pad_maximum_fusion
  1055.3 75.1 %psum.71 = f32[2,6912]{1,0:T(2,128)S(1)} all-reduce(f32[2,6912]{1,0:T(2,128)S(1)} %pad_maximum_fusion.10), channel_id=1, replica_groups=mesh['dp'=16,'tensor'=2] {'dp'}, use_global_device_ids=true, to_apply=%region_56.57 | all-reduce | flops 13824 | bytes 110592 | tf_op jit(solution)/shard_map/psum | solution.py:488
  1131.1 5.9 add_convert_fusion
  (616 shorter events, 318.9 us)
Async XLA Ops:
  7.2 71.8 %all-reduce.9.cloned.1.call-start = ((), (), s32[]{:S(2)}) async-start(), calls=%async_computation | async-start | bytes 6291456 | tf_op jit(solution)/shard_map/psum | solution.py:448
  11.8 70.7 %copy-start.73 = (f32[768]{0:T(1024)}, f32[768]{0:T(1024)S(1)}, u32[]{:S(2)}) copy-start(f32[768]{0:T(1024)S(1)} %get-tuple-element.624) | copy-start | bytes 9220
  11.8 70.7 %copy-start.130 = (f32[768]{0:T(1024)}, f32[768]{0:T(1024)S(1)}, u32[]{:S(2)}) copy-start(f32[768]{0:T(1024)S(1)} %get-tuple-element.478) | copy-start | bytes 9220
  48.0 34.5 %copy-start.60 = (f32[2,6,512]{2,1,0:T(8,128)}, f32[2,6,512]{2,1,0:T(8,128)S(1)}, u32[]{:S(2)}) copy-start(f32[2,6,512]{2,1,0:T(8,128)S(1)} %get-tuple-element.1000) | copy-start | bytes 73732
  52.9 67.6 %all-reduce.11.cloned.1.call-start = ((), (), s32[]{:S(2)}) async-start(), calls=%async_computation.1 | async-start | bytes 6291456 | tf_op jit(solution)/shard_map/psum | solution.py:448
  54.8 32.8 %copy-start.119 = (f32[1536]{0:T(1024)}, f32[1536]{0:T(1024)S(1)}, u32[]{:S(2)}) copy-start(f32[1536]{0:T(1024)S(1)} %get-tuple-element.472) | copy-start | bytes 18436
  79.0 11.3 slice-start.8
  82.0 38.5 %copy-start.8 = (f32[1024,768]{1,0:T(8,128)}, f32[1024,768]{1,0:T(8,128)S(1)}, u32[]{:S(2)}) copy-start(f32[1024,768]{1,0:T(8,128)S(1)} %get-tuple-element.584) | copy-start | bytes 9437188
  82.5 7.7 slice-start.9
  95.9 92.1 %all-reduce.13.cloned.1.call-start = ((), (), s32[]{:S(2)}) async-start(), calls=%async_computation.2 | async-start | bytes 6291456 | tf_op jit(solution)/shard_map/psum | solution.py:448
  160.8 27.3 %copy-start.104 = (f32[768]{0:T(1024)S(1)}, f32[768]{0:T(1024)}, u32[]{:S(2)}) copy-start(f32[768]{0:T(1024)} %get-tuple-element.470) | copy-start | bytes 9220
  163.5 73.4 %all-reduce.15.cloned.1.call-start = ((), (), s32[]{:S(2)}) async-start(), calls=%async_computation.3 | async-start | bytes 6291456 | tf_op jit(solution)/shard_map/psum | solution.py:452
  188.1 9.1 slice-start.10
  191.5 50.0 %copy-start.71 = (f32[1024]{0:T(1024)}, f32[1024]{0:T(1024)S(1)}, u32[]{:S(2)}) copy-start(f32[1024]{0:T(1024)S(1)} %broadcast_multiply_fusion) | copy-start | bytes 12292
  192.1 49.5 %copy-start.89 = (f32[1024]{0:T(1024)}, f32[1024]{0:T(1024)S(1)}, u32[]{:S(2)}) copy-start(f32[1024]{0:T(1024)S(1)} %fusion.164) | copy-start | bytes 12292
  192.2 15.8 %slice-start.14 = ((s8[4718592]{0:T(1024)(128)(4,1)}), s8[4194304]{0:T(1024)(128)(4,1)S(1)}, s32[]{:S(2)}) async-start(s8[4718592]{0:T(1024)(128)(4,1)} %bitcast.412), calls=%async_computation.21 | async-start | bytes 8388608
  197.1 9.3 copy-start.139
  197.2 10.9 slice-start.15
  212.4 150.6 %all-reduce.17.cloned.1.call-start = ((), (), s32[]{:S(2)}) async-start(), calls=%async_computation.4 | async-start | bytes 6291456 | tf_op jit(solution)/shard_map/psum | solution.py:452
  321.1 114.6 %all-reduce.19.cloned.1.call-start = ((), (), s32[]{:S(2)}) async-start(), calls=%async_computation.5 | async-start | bytes 6291456 | tf_op jit(solution)/shard_map/psum | solution.py:452
  339.6 7.5 copy-start.6
  339.6 7.5 copy-start.72
  339.6 7.5 copy-start.79
  339.6 7.5 copy-start.90
  339.6 7.5 copy-start.135
  353.6 9.3 copy-start.12
  353.6 9.3 copy-start.70
  353.6 9.3 copy-start.77
  353.6 9.3 copy-start.86
  368.4 12.3 %slice-start.16 = ((s8[4718592]{0:T(1024)(128)(4,1)}), s8[4194304]{0:T(1024)(128)(4,1)S(1)}, s32[]{:S(2)}) async-start(s8[4718592]{0:T(1024)(128)(4,1)} %bitcast.414), calls=%async_computation.23 | async-start | bytes 8388608
  369.8 9.2 copy-start.20
  370.5 10.2 slice-start.17
  385.0 664.3 %all-reduce.21.cloned.1.call-start = ((), (), s32[]{:S(2)}) async-start(), calls=%async_computation.6 | async-start | bytes 12582912 | tf_op jit(solution)/shard_map/psum | solution.py:448
  426.6 9.1 copy-start.9
  426.6 9.1 copy-start.67
  426.6 9.1 copy-start.74
  426.6 9.2 copy-start.83
  506.6 7.9 copy-start.58
  521.5 7.5 copy-start.68
  521.5 7.5 copy-start.75
  521.5 7.5 copy-start.84
  521.6 7.5 copy-start.131
  1030.1 7.8 slice-start.2
  1030.1 7.8 slice-start.4
  1033.9 8.5 slice-start.6
  1052.0 79.0 %copy-start.88 = (f32[1024]{0:T(1024)S(1)}, f32[1024]{0:T(1024)}, u32[]{:S(2)}) copy-start(f32[1024]{0:T(1024)} %copy-done.87) | copy-start | bytes 12292
  1131.1 8.4 copy-start.7
  1131.1 8.4 copy-start.103
  (129 other events, 400.3 us)
Sparse Core Ops, SparseCore 0:
  53.0 25.8 all-reduce.8
  96.0 24.4 all-reduce.10
  163.6 24.3 all-reduce.12
  212.5 24.3 all-reduce.14
  321.2 24.3 all-reduce.16
  385.1 24.3 all-reduce.18
  514.7 33.1 all-reduce.20

commit v2 on v1

--- a/solution.py
+++ b/solution.py
@@ -4,6 +4,12 @@
 from jax.experimental import pallas as pl
 from jax.experimental.pallas import tpu as pltpu
 from jax.sharding import PartitionSpec as P
+
+HEAD_DIM = 64
+LEN = 1024
+LAYERS = 2
+UNIT = 384
+BLOCK = 16
 MESH = pl.DeviceIdType.MESH
 
 
@@ -259,10 +265,11 @@
             self.own_copy(g).start()
         elif e in (6, 7):
             self.finish_gather(e - 5, g)
+            if e == 6:
+                self.own_copy(g).wait()
             self.start_gather(e - 4, g)
         elif e == 8:
             self.finish_gather(3, g)
-            self.own_copy(g).wait()
             self.last(g).start()
         else:
             copy = self.last(g)
@@ -297,37 +304,433 @@
         return self.target.at[g, :, pl.ds(pl.multiple_of(start, 8), size)]
 
 
-def all_reduce(flat, slots=4, lags=(2, 1, 1, 1, 1, 1, 1, 1, 2)):
-    groups, _, rows, cols = flat.shape
-    plan = FlatExchange(groups, rows, cols, slots, lags)
-    scratch = plan.scratch()
+ROWS = 256
+
+
+def dot(a, b, dims):
+    return lax.dot_general(a, b, (dims, ((), ())), preferred_element_type=jnp.float32)
+
+
+NN = ((1,), (0,))
+NT = ((1,), (1,))
+TN = ((0,), (0,))
+
+
+def gelu_slope(x):
+    t = jnp.tanh(0.7978845608028654 * (x + 0.044715 * x * x * x))
+    return 0.5 * (1.0 + t) + 0.5 * x * (1.0 - t * t) * (
+        0.7978845608028654 * (1.0 + 3.0 * 0.044715 * x * x)
+    )
+
+
+def norm_parts(h):
+    centre = h - jnp.mean(h, axis=-1, keepdims=True)
+    r = lax.rsqrt(jnp.mean(centre * centre, axis=-1, keepdims=True) + 1e-05)
+    return centre * r, r
+
+
+GAIN, SHIFT, BRANCH, HIDDEN, OFFSETS, SMALL = 0, 2, 4, 6, 8, 16
+PIECES = 9
+PER_LAYER = 12
+
+
+class Backward(FlatExchange):
+    LOADS = ("act", "pre", "norm", "h", "att", "q", "k", "v", "w_shrink", "w_expand", "w_merge", "w_heads")
+
+    def more_scratch(self):
+        T, D, W, F = self.T, self.D, self.W, self.F
+        low, full = jnp.bfloat16, jnp.float32
+        dma = pltpu.SemaphoreType.DMA
+        return dict(
+            act=pltpu.VMEM((T, F), low), pre=pltpu.VMEM((T, F), full), norm=pltpu.VMEM((T, D), low),
+            h=pltpu.VMEM((T, D), full), att=pltpu.VMEM((T, W), low), q=pltpu.VMEM((T, W), low),
+            k=pltpu.VMEM((T, W), low), v=pltpu.VMEM((T, W), low), w_shrink=pltpu.VMEM((F, D), low),
+            w_expand=pltpu.VMEM((D, F), low), w_merge=pltpu.VMEM((W, D), low), w_heads=pltpu.VMEM((3, D, W), low),
+            g=pltpu.VMEM((T, D), full), low=pltpu.VMEM((T, D), low), came=pltpu.VMEM((T, D), full),
+            datt=pltpu.VMEM((T, W), low), dqkv=pltpu.VMEM((3, T, W), low),
+            staged=pltpu.VMEM((2, 2, 384, 384), full), dk=pltpu.VMEM((T, 128), full), dv=pltpu.VMEM((T, 128), full),
+            small=pltpu.VMEM((2 * SMALL, D), full), small_in=pltpu.VMEM((4, 2 * SMALL, D), full),
+            input_s=dma((len(self.LOADS),)), cot_s=dma, staged_s=dma((2,)), tokens_s=dma,
+            core_s=dma((T // ROWS,)), core_r=dma((T // ROWS,)), core_c=pltpu.SemaphoreType.REGULAR,
+            small_s=dma((4,)), small_r=dma((4,)),
+        )
+
+    def held_slots(self):
+        return self.starts[6]
+
+    def held(self, g):
+        return self.refs["held"].at[lax.rem(g, self.held_slots())]
+
+    def fetch(self, name, layer, second=False):
+        source = self.inputs[name][layer]
+        if name in ("norm", "h"):
+            source = source[1 if second else 0]
+        pltpu.make_async_copy(source, self.refs[name], self.refs["input_s"].at[self.LOADS.index(name)]).start()
+
+    def arrive(self, name):
+        source = self.inputs[name][0]
+        if name in ("norm", "h"):
+            source = source[0]
+        pltpu.make_async_copy(source, self.refs[name], self.refs["input_s"].at[self.LOADS.index(name)]).wait()
+
+    def fetch_next(self, l, *names, second=False):
+        @pl.when(l == 1)
+        def _():
+            for name in names:
+                self.fetch(name, 0, second)
+
+    def stage_copy(self, at, g):
+        return pltpu.make_async_copy(self.refs["staged"].at[at], self.source.at[g], self.refs["staged_s"].at[at])
+
+    def put(self, at, g, top, bottom):
+        self.refs["staged"][at, 0] = top
+        self.refs["staged"][at, 1] = bottom
+        self.stage_copy(at, g).start()
+
+    def outer(self, left, left_cols, right, right_cols, at, g):
+        for u in range(2):
+            a = left[:, pl.ds(pl.multiple_of(left_cols + u * 384, 128), 384)]
+            self.refs["staged"][at, u] = dot(a, right[:, right_cols], TN)
+        self.stage_copy(at, g).start()
+
+    def core_copy(self, i):
+        r = self.refs
+        rows = pl.ds(pl.multiple_of(i * ROWS, ROWS), ROWS)
+        return self.copy(
+            r["pre"].at[rows, pl.ds(0, self.D)], r["came"].at[rows], r["core_s"].at[i], r["core_r"].at[i],
+            (self.dp, 1 - self.core),
+        )
+
+    def partial(self, make, wait):
+        @pl.when(wait)
+        def _():
+            pl.semaphore_wait(self.refs["core_c"], 1)
+
+        def block(i, carry):
+            rows = pl.ds(pl.multiple_of(i * ROWS, ROWS), ROWS)
+            self.refs["pre"][rows, 0 : self.D] = make(rows)
+            self.core_copy(i).start()
+            return carry
+
+        lax.fori_loop(0, self.T // ROWS, block, 0)
+
+    def norm_back(self, l, which, more, after):
+        r, D = self.refs, self.D
+        gain = self.gain[l, which]
+        n = 128
+        blocks = ROWS // n
+
+        def block(i, carry):
+            @pl.when(lax.rem(i, blocks) == 0)
+            def _():
+                copy = self.core_copy(lax.div(i, blocks))
+                copy.wait_send()
+                copy.wait_recv()
+
+            rows = pl.ds(pl.multiple_of(i * n, n), n)
+            xhat, rstd = norm_parts(r["h"][rows])
+            d = r["pre"][rows, 0:D] + r["came"][rows]
+            e = d * gain
+            spread = xhat * jnp.mean(e * xhat, axis=-1, keepdims=True)
+            new = r["g"][rows] + rstd * (e - jnp.mean(e, axis=-1, keepdims=True) - spread)
+            r["g"][rows] = new
+            rounded = new.astype(jnp.bfloat16)
+            r["low"][rows] = rounded
+            return (
+                carry[0] + jnp.sum(d * xhat, axis=0, keepdims=True),
+                carry[1] + jnp.sum(d, axis=0, keepdims=True),
+                carry[2] + jnp.sum(rounded.astype(jnp.float32), axis=0, keepdims=True),
+            )
+
+        zero = jnp.zeros((1, D), jnp.float32)
+        sums = lax.fori_loop(0, self.T // n, block, (zero, zero, zero))
+        self.row(l, GAIN + which)[...] = sums[0]
+        self.row(l, SHIFT + which)[...] = sums[1]
+        after(sums[2])
+
+        @pl.when(more)
+        def _():
+            pl.semaphore_signal(
+                r["core_c"], inc=1, device_id=(self.dp, 1 - self.core), device_id_type=MESH
+            )
+
+    def row(self, l, at, start=0, size=None):
+        size = self.D if size is None else size
+        return self.refs["small"].at[pl.ds(l * SMALL + at, 1), start : start + size]
+
+    def piece(self, p, l):
+        r = self.refs
+        T, D, W, F = self.T, self.D, self.W, self.F
+        base = (1 - l) * PER_LAYER
+        if p == 0:
+            @pl.when(l == 1)
+            def _():
+                pltpu.make_async_copy(self.cotangent, r["low"], r["cot_s"]).wait()
+
+                def widen(i, carry):
+                    rows = pl.ds(pl.multiple_of(i * ROWS, ROWS), ROWS)
+                    wide = r["low"][rows].astype(jnp.float32)
+                    r["g"][rows] = wide
+                    return carry + jnp.sum(wide, axis=0, keepdims=True)
+
+                self.row(l, BRANCH + 1)[...] = lax.fori_loop(0, T // ROWS, widen, jnp.zeros((1, D), jnp.float32))
+
+            self.arrive("act")
+
+            def one(i, carry):
+                at = lax.rem(i, 2)
+
+                @pl.when(i >= 2)
+                def _():
+                    self.stage_copy(at, base + i - 2).wait()
+
+                self.outer(r["act"], lax.div(i, 2) * 768, r["low"], pl.ds(pl.multiple_of(at * 384, 128), 384), at, base + i)
+                return carry
+
+            lax.fori_loop(0, 4, one, 0)
+            for i in (2, 3):
+                self.stage_copy(i % 2, base + i).wait()
+        elif p == 1:
+            self.arrive("w_shrink")
+            self.arrive("pre")
+
+            def one(i, carry):
+                rows = pl.ds(pl.multiple_of(i * ROWS, ROWS), ROWS)
+                sums = []
+                for c in range(0, F, 512):
+                    d_act = dot(r["low"][rows], r["w_shrink"][c : c + 512], NT)
+                    d_pre = (d_act * gelu_slope(r["pre"][rows, c : c + 512])).astype(jnp.bfloat16)
+                    r["act"][rows, c : c + 512] = d_pre
+                    sums.append(carry[c // 512] + jnp.sum(d_pre.astype(jnp.float32), axis=0, keepdims=True))
+                return tuple(sums)
+
+            sums = lax.fori_loop(0, T // ROWS, one, (jnp.zeros((1, 512), jnp.float32),) * (F // 512))
+            for i, part in enumerate(sums):
+                for j in range(2):
+                    at = i * 512 + j * 256
+                    self.row(l, HIDDEN + at // D, at % D, 256)[...] = part[:, j * 256 : (j + 1) * 256]
+            self.fetch_next(l, "w_shrink")
+        elif p == 2:
+            self.arrive("w_expand")
+            self.partial(lambda rows: dot(r["act"][rows], r["w_expand"][...], NT), l == 0)
+            self.arrive("norm")
+
+            def one(i, carry):
+                at = lax.rem(i, 2)
+
+                @pl.when(i >= 2)
+                def _():
+                    self.stage_copy(at, base + 4 + i - 2).wait()
+
+                self.outer(r["norm"], 0, r["act"], pl.ds(pl.multiple_of(i * 384, 128), 384), at, base + 4 + i)
+                return carry
+
+            lax.fori_loop(0, 4, one, 0)
+            for i in (2, 3):
+                self.stage_copy(i % 2, base + 4 + i).wait()
+            self.fetch_next(l, "w_expand", "act")
+            for layer in range(2):
+                @pl.when(l == layer)
+                def _():
+                    self.fetch("norm", layer)
+        elif p == 3:
+            self.arrive("h")
+
+            def after(total):
+                self.row(l, BRANCH)[...] = total
+
+            self.norm_back(l, 1, jnp.bool_(True), after)
+            for layer in range(2):
+                @pl.when(l == layer)
+                def _():
+                    self.fetch("h", layer)
+
+            self.arrive("w_merge")
+            self.arrive("att")
+
+            def one(i, carry):
+                rows = pl.ds(pl.multiple_of(i * ROWS, ROWS), ROWS)
+                r["datt"][rows] = dot(r["low"][rows], r["w_merge"][...], NT).astype(jnp.bfloat16)
+                return carry
+
+            lax.fori_loop(0, T // ROWS, one, 0)
+            for u in range(2):
+                r["staged"][0, u] = dot(r["att"][...], r["low"][:, u * 384 : (u + 1) * 384], TN)
+            self.stage_copy(0, base + 8).start()
+            self.stage_copy(0, base + 8).wait()
+            self.fetch_next(l, "w_merge", "att")
+            self.arrive("q")
+            self.arrive("k")
+            self.arrive("v")
+        elif p in (4, 5, 6):
+            self.attend_back(p - 4, l)
+            if p == 6:
+                self.fetch_next(l, "q", "k", "v")
+        elif p == 7:
+            self.arrive("w_heads")
+
+            def make(rows):
+                total = dot(r["dqkv"][0, rows], r["w_heads"][0], NT)
+                for c in (1, 2):
+                    total = total + dot(r["dqkv"][c, rows], r["w_heads"][c], NT)
+                return total
+
+            self.partial(make, jnp.bool_(True))
+            self.arrive("norm")
+            for c in range(3):
+                at = c % 2
+                if c == 2:
+                    self.stage_copy(at, base + 9).wait()
+                for u in range(2):
+                    r["staged"][at, u] = dot(r["norm"][:, u * 384 : (u + 1) * 384], r["dqkv"][c], TN)
+                self.stage_copy(at, base + 9 + c).start()
+            for c in (1, 2):
+                self.stage_copy(c % 2, base + 9 + c).wait()
+            for i, c in enumerate((0, 2)):
+                self.row(l, OFFSETS, i * W, W)[...] = jnp.sum(r["dqkv"][c].astype(jnp.float32), axis=0, keepdims=True)
+            self.fetch_next(l, "w_heads")
+            self.fetch_next(l, "norm", second=True)
+        else:
+            self.arrive("h")
+
+            def after(total):
+                @pl.when(l == 1)
+                def _():
+                    self.row(0, BRANCH + 1)[...] = total
+
+            self.norm_back(l, 0, l == 1, after)
+            self.fetch_next(l, "pre")
+            self.fetch_next(l, "h", second=True)
+
+            @pl.when(l == 0)
+            def _():
+                pltpu.make_async_copy(r["low"], self.grad_tokens, r["tokens_s"]).start()
+
+    def attend_back(self, pair, l):
+        r = self.refs
+        T = self.T
+        lanes = pl.ds(pl.multiple_of(pair * 128, 128), 128)
+        r["dk"][...] = jnp.zeros((T, 128), jnp.float32)
+        r["dv"][...] = jnp.zeros((T, 128), jnp.float32)
+        lane = lax.broadcasted_iota(jnp.int32, (1, 128), 1)
+        for b in range(T // ROWS):
+            rows, end = slice(b * ROWS, (b + 1) * ROWS), (b + 1) * ROWS
+            query = b * ROWS + lax.broadcasted_iota(jnp.int32, (1, ROWS), 1)
+            lowest = query - self.positions[:, rows]
+            key = lax.broadcasted_iota(jnp.int32, (end, ROWS), 0)
+            allowed = (key <= query) & (key >= lowest)
+            q, d = r["q"][rows, lanes], r["datt"][rows, lanes]
+            k, v = r["k"][0:end, lanes], r["v"][0:end, lanes]
+            dq = jnp.zeros((ROWS, 128), jnp.float32)
+            for side in range(2):
+                mine = (lax.div(lane, 64) == side).astype(jnp.float32).astype(jnp.bfloat16)
+                q_own, d_own = q * mine, d * mine
+                scores = dot(k, q_own, NT) * 0.125
+                lse = self.lse[l, pl.ds(pair * 2 + side, 1), rows]
+                probs = jnp.where(allowed, jnp.exp(scores - lse), 0.0)
+                dprob = dot(v, d_own, NT)
+                centre = jnp.sum(probs * dprob, axis=0, keepdims=True)
+                dscore = (probs * (dprob - centre)).astype(jnp.bfloat16)
+                r["dv"][0:end] = r["dv"][0:end] + dot(probs.astype(jnp.bfloat16), d_own, NN)
+                r["dk"][0:end] = r["dk"][0:end] + dot(dscore, q_own, NN)
+                dq = dq + dot(dscore, k * mine, TN)
+            r["dqkv"][0, rows, lanes] = (dq * 0.125).astype(jnp.bfloat16)
+        r["dqkv"][1, :, lanes] = (r["dk"][...] * 0.125).astype(jnp.bfloat16)
+        r["dqkv"][2, :, lanes] = r["dv"][...].astype(jnp.bfloat16)
+
+    def small_swap(self, step):
+        r = self.refs
+        z = self.z
+        to = (
+            self.dp + self.step_x,
+            self.dp + self.step_y,
+            self.dp + 4 - 8 * lax.rem(z, 2),
+            self.dp + 8 - 16 * lax.div(z, 2),
+        )[step]
+        return self.copy(
+            r["small"], r["small_in"].at[step], r["small_s"].at[step], r["small_r"].at[step], (to, self.core)
+        )
+
+    def small_stage(self, step):
+        if step > 0:
+            copy = self.small_swap(step - 1)
+            copy.wait_send()
+            copy.wait_recv()
+            self.refs["small"][...] = self.refs["small"][...] + self.refs["small_in"][step - 1]
+        if step < 4:
+            self.small_swap(step).start()
+
+    def run(self):
+        r = self.refs
+        pltpu.make_async_copy(self.cotangent, r["low"], r["cot_s"]).start()
+        for name in self.LOADS:
+            self.fetch(name, 1, second=True)
+        r["small"][...] = jnp.zeros(r["small"].shape, jnp.float32)
+        far = (self.dp + 8 - 16 * lax.div(self.z, 2), self.core)
+        self.barrier(((self.dp, 1 - self.core), far))
+
+        def step(t, carry):
+            l = 1 - lax.div(t, PIECES)
+            for p in range(PIECES):
+                @pl.when((lax.rem(t, PIECES) == p) & (t < 2 * PIECES))
+                def _():
+                    self.piece(p, l)
+
+            for s in range(5):
+                @pl.when(t == 2 * PIECES + s)
+                def _():
+                    self.small_stage(s)
+
+            self.tick(t)
+            return carry
+
+        lax.fori_loop(0, self.ticks, step, 0)
+        pltpu.make_async_copy(r["low"], self.grad_tokens, r["tokens_s"]).wait()
+        self.small_out[...] = r["small"][...]
+
+
+def backward(layers, weights, gain, lse, positions, cotangent, slots=4, lags=(2, 1, 1, 1, 1, 1, 1, 1, 2)):
+    T, F = layers[0]["act"].shape
+    D, W = cotangent.shape[1], layers[0]["q"].shape[1]
+    groups = 2 * PER_LAYER
+    plan = Backward(groups, 384, 384, slots, lags)
+    plan.T, plan.D, plan.W, plan.F = T, D, W, F
+    scratch = plan.scratch() | plan.more_scratch()
     names = list(scratch)
-
-    def kernel(source, target, *refs):
-        plan.source, plan.target = source, target
-        plan.setup(dict(zip(names, refs)))
-        plan.barrier()
-
-        def step(t, carry):
-            plan.tick(t)
-            return carry
-
-        lax.fori_loop(0, plan.ticks, step, 0)
-
-    return pl.pallas_call(
+    tree = dict(layers=layers, weights=weights, cotangent=cotangent)
+    flat_inputs, shape = jax.tree.flatten(tree)
+    n = len(flat_inputs)
+
+    def kernel(*refs):
+        held = jax.tree.unflatten(shape, refs[:n])
+        plan.gain, plan.lse, plan.positions = refs[n : n + 3]
+        plan.target, plan.source, plan.grad_tokens, plan.small_out = refs[n + 3 : n + 7]
+        plan.setup(dict(zip(names, refs[n + 7 :])))
+        plan.cotangent = held["cotangent"]
+        plan.inputs = {name: [held["layers"][i][name] for i in range(2)] for name in ("act", "pre", "norm", "h", "att", "q", "k", "v")}
+        for name in ("shrink", "expand", "merge", "heads"):
+            plan.inputs["w_" + name] = [held["weights"][name].at[i] for i in range(2)]
+        plan.run()
+
+    hbm = pl.BlockSpec(memory_space=pl.ANY)
+    vmem = pl.BlockSpec(memory_space=pltpu.VMEM)
+    flat = jax.ShapeDtypeStruct((groups, 2, 384, 384), jnp.float32)
+    target, _, grad_tokens, small = pl.pallas_call(
         kernel,
-        out_shape=jax.ShapeDtypeStruct(flat.shape, jnp.float32),
-        in_specs=[pl.BlockSpec(memory_space=pl.ANY)],
-        out_specs=pl.BlockSpec(memory_space=pl.ANY),
-        scratch_shapes=[scratch[n] for n in names],
-        compiler_params=pltpu.CompilerParams(collective_id=0, has_side_effects=True, vmem_limit_bytes=60 * 2**20),
-    )(flat)
-
-
-HEAD_DIM = 64
-LEN = 1024
-LAYERS = 2
-UNIT = 384
+        out_shape=(
+            flat,
+            flat,
+            jax.ShapeDtypeStruct((T, D), jnp.bfloat16),
+            jax.ShapeDtypeStruct((2 * SMALL, D), jnp.float32),
+        ),
+        in_specs=[hbm] * n + [vmem] * 3,
+        out_specs=(hbm, hbm, hbm, vmem),
+        scratch_shapes=[scratch[name] for name in names],
+        compiler_params=pltpu.CompilerParams(
+            collective_id=0, has_side_effects=True, vmem_limit_bytes=61 * 2**20
+        ),
+    )(*flat_inputs, gain, lse, positions)
+    return target, grad_tokens, small
 
 
 def layer_norm(stream, gain_row, shift_row):
@@ -386,129 +789,8 @@
     return (blended.reshape(length, local_heads, HEAD_DIM), logsum)
 
 
-def attend_back(query_rows, key_rows, value_rows, offsets_row, logsum, grad_blended):
-    length = query_rows.shape[0]
-    local_heads = query_rows.shape[1]
-    stride = min(512, length)
-    pieces = length // stride
-
-    def one_block(running, record):
-        grad_keys, grad_values = running
-        position, query_part, offset_part, logsum_part, grad_part = record
-        scores = (
-            jnp.einsum("qhd,khd->hqk", query_part, key_rows, preferred_element_type=jnp.float32)
-            * 0.125
-        )
-        allowed = block_mask(position * stride, stride, offset_part, length)
-        chances = jnp.where(allowed[None], jnp.exp(scores - logsum_part[:, :, None]), 0.0)
-        grad_chances = jnp.einsum(
-            "qhd,khd->hqk", grad_part, value_rows, preferred_element_type=jnp.float32
-        )
-        centre = jnp.sum(chances * grad_chances, axis=-1, keepdims=True)
-        grad_scores = (chances * (grad_chances - centre)).astype(jnp.bfloat16)
-        grad_query = (
-            jnp.einsum("hqk,khd->qhd", grad_scores, key_rows, preferred_element_type=jnp.float32)
-            * 0.125
-        )
-        grad_keys = (
-            grad_keys
-            + jnp.einsum(
-                "hqk,qhd->khd", grad_scores, query_part, preferred_element_type=jnp.float32
-            )
-            * 0.125
-        )
-        grad_values = grad_values + jnp.einsum(
-            "hqk,qhd->khd",
-            chances.astype(jnp.bfloat16),
-            grad_part,
-            preferred_element_type=jnp.float32,
-        )
-        return ((grad_keys, grad_values), grad_query.astype(jnp.bfloat16))
-
-    empty = jnp.zeros((length, local_heads, HEAD_DIM), jnp.float32)
-    (grad_keys, grad_values), grad_query = lax.scan(
-        one_block,
-        (empty, empty),
-        (
-            jnp.arange(pieces, dtype=jnp.int32),
-            query_rows.reshape(pieces, stride, local_heads, HEAD_DIM),
-            offsets_row.reshape(pieces, stride),
-            logsum,
-            grad_blended.reshape(pieces, stride, local_heads, HEAD_DIM),
-        ),
-    )
-    return (
-        grad_query.reshape(length, local_heads, HEAD_DIM),
-        grad_keys.astype(jnp.bfloat16),
-        grad_values.astype(jnp.bfloat16),
-    )
-
-
 def add_branch(stream, partial_sum, bias_row):
     return stream + (lax.psum(partial_sum, "tensor") + bias_row)
-
-
-def reduce_inputs(partial_sum):
-    return lax.psum(partial_sum, "tensor")
-
-
-BLOCK = 16
-
-
-def columns_to_units(matrix):
-    rows, width = matrix.shape
-    return matrix.reshape(rows, width // UNIT, UNIT).transpose(1, 0, 2)
-
-
-def units_to_columns(units):
-    count, rows, width = units.shape
-    return units.transpose(1, 0, 2).reshape(rows, count * width)
-
-
-def reduce_grads(layers):
-    ranks = lax.axis_size("dp")
-    small = jnp.stack([jnp.concatenate([layer[m].reshape(-1) for m in (0, 1, 3, 5, 7)]) for layer in layers])
-    pieces = []
-    for layer in reversed(layers):
-        heads, merge, expand, shrink = layer[2], layer[4], layer[6], layer[8]
-        depth = expand.shape[0]
-        pieces.append(columns_to_units(shrink).reshape(shrink.shape[1] // UNIT, -1, UNIT, UNIT).transpose(1, 0, 2, 3).reshape(-1, UNIT, UNIT))
-        pieces.append(columns_to_units(expand).reshape(-1, UNIT, UNIT))
-        pieces.append(columns_to_units(merge))
-        pieces.append(heads.reshape(-1, UNIT, UNIT))
-    flat = jnp.concatenate(pieces)
-    flat = flat.reshape(flat.shape[0] // 2, 2, UNIT, UNIT)
-    if ranks % BLOCK:
-        flat = lax.psum(flat, "dp")
-    else:
-        flat = all_reduce(flat)
-        if ranks > BLOCK:
-            groups = [[j * BLOCK + i for j in range(ranks // BLOCK)] for i in range(BLOCK)]
-            flat = lax.psum(flat, "dp", axis_index_groups=groups)
-    small = lax.psum(small, "dp")
-    flat = flat.reshape(-1, UNIT, UNIT)
-    out = []
-    at = 0
-    for layer in reversed(layers):
-        heads, merge, expand, shrink = layer[2], layer[4], layer[6], layer[8]
-        def take(like):
-            nonlocal at
-            n = like.size // (UNIT * UNIT)
-            at += n
-            return flat[at - n : at]
-        shrink_sum = take(shrink).reshape(-1, shrink.shape[1] // UNIT, UNIT, UNIT).transpose(0, 2, 1, 3).reshape(shrink.shape)
-        expand_sum = units_to_columns(take(expand).reshape(-1, expand.shape[0], UNIT))
-        merge_sum = units_to_columns(take(merge))
-        heads_sum = take(heads).reshape(heads.shape)
-        out.append((heads_sum, merge_sum, expand_sum, shrink_sum))
-    out = [jnp.stack(group) for group in zip(*reversed(out))]
-    smalls = []
-    at = 0
-    for m in (0, 1, 3, 5, 7):
-        like = layers[0][m]
-        smalls.append(small[:, at : at + like.size].reshape((len(layers),) + like.shape))
-        at += like.size
-    return (smalls[0], smalls[1], out[0], smalls[2], out[1], smalls[3], out[2], smalls[4], out[3])
 
 
 def to_heads(matrix, sequences, local_heads):
@@ -535,7 +817,7 @@
     sequences = row_count // LEN
     offsets_rows = positions.reshape(sequences, LEN)
     stream = tokens.astype(jnp.float32)
-    kept_values = []
+    kept, lses = [], []
     for layer_index in range(LAYERS):
         normed = layer_norm(stream, norm_gain[layer_index, 0], norm_shift[layer_index, 0]).astype(
             jnp.bfloat16
@@ -571,141 +853,42 @@
         partial_sum = jnp.dot(
             active, shrink_weight[layer_index], preferred_element_type=jnp.float32
         )
-        kept_values.append(
-            (
-                stream,
-                normed,
-                query_rows,
-                key_rows,
-                value_rows,
-                logsum,
-                blended_rows,
-                middle,
-                normed_two,
-                hidden,
-                active,
+        kept.append(
+            dict(
+                act=active, pre=hidden, norm=(normed, normed_two), h=(stream, middle), att=blended_rows,
+                q=query_rows, k=key_rows, v=value_rows,
             )
         )
+        lses.append(jnp.pad(logsum[0].transpose(1, 0, 2).reshape(local_heads, row_count), ((0, 2), (0, 0))))
         stream = add_branch(middle, partial_sum, branch_bias[layer_index, 1])
     output = stream.astype(jnp.bfloat16)
-    upstream = cotangent.astype(jnp.float32)
-    layer_grads = [None] * LAYERS
-    for layer_index in reversed(range(LAYERS)):
-        (
-            stream_in,
-            normed,
-            query_rows,
-            key_rows,
-            value_rows,
-            logsum,
-            blended_rows,
-            middle,
-            normed_two,
-            hidden,
-            active,
-        ) = kept_values[layer_index]
-        grad_second = upstream.astype(jnp.bfloat16)
-        bias_second = jnp.sum(grad_second, axis=0, dtype=jnp.float32)
-        shrink_grad = jnp.einsum(
-            "tf,td->fd", active, grad_second, preferred_element_type=jnp.float32
-        )
-        grad_active = jnp.einsum(
-            "td,fd->tf", grad_second, shrink_weight[layer_index], preferred_element_type=jnp.float32
-        )
-        _, gelu_pullback = jax.vjp(gelu_tanh, hidden)
-        grad_pre = gelu_pullback(grad_active)[0].astype(jnp.bfloat16)
-        hidden_grad = jnp.sum(grad_pre, axis=0, dtype=jnp.float32)
-        expand_grad = jnp.einsum(
-            "td,tf->df", normed_two, grad_pre, preferred_element_type=jnp.float32
-        )
-        grad_normed_two = reduce_inputs(
-            jnp.einsum(
-                "tf,df->td",
-                grad_pre,
-                expand_weight[layer_index],
-                preferred_element_type=jnp.float32,
-            )
-        )
-        _, norm_pullback = jax.vjp(
-            layer_norm, middle, norm_gain[layer_index, 1], norm_shift[layer_index, 1]
-        )
-        grad_middle, gain_second, shift_second = norm_pullback(grad_normed_two)
-        grad_middle = grad_middle + upstream
-        grad_first = grad_middle.astype(jnp.bfloat16)
-        bias_first = jnp.sum(grad_first, axis=0, dtype=jnp.float32)
-        merge_grad = jnp.einsum(
-            "te,td->ed", blended_rows, grad_first, preferred_element_type=jnp.float32
-        )
-        grad_blended = jnp.einsum(
-            "td,ed->te", grad_first, merge_weight[layer_index], preferred_element_type=jnp.float32
-        ).astype(jnp.bfloat16)
-        grad_query, grad_keys, grad_values = lax.map(
-            lambda record: attend_back(
-                record[0], record[1], record[2], record[3], record[4], record[5]
-            ),
-            (
-                to_heads(query_rows, sequences, local_heads),
-                to_heads(key_rows, sequences, local_heads),
-                to_heads(value_rows, sequences, local_heads),
-                offsets_rows,
-                logsum,
-                to_heads(grad_blended, sequences, local_heads),
-            ),
-        )
-        grad_stack = jnp.stack(
-            [
-                grad_query.reshape(row_count, local_width),
-                grad_keys.reshape(row_count, local_width),
-                grad_values.reshape(row_count, local_width),
-            ]
-        )
-        heads_grad = jnp.einsum(
-            "td,cte->cde", normed, grad_stack, preferred_element_type=jnp.float32
-        )
-        offsets_grad = jnp.stack(
-            [
-                jnp.sum(grad_stack[0], axis=0, dtype=jnp.float32),
-                jnp.sum(grad_stack[2], axis=0, dtype=jnp.float32),
-            ]
-        )
-        grad_normed = reduce_inputs(
-            jnp.einsum(
-                "cte,cde->td",
-                grad_stack,
-                heads_weight[layer_index],
-                preferred_element_type=jnp.float32,
-            )
-        )
-        _, norm_pullback = jax.vjp(
-            layer_norm, stream_in, norm_gain[layer_index, 0], norm_shift[layer_index, 0]
-        )
-        grad_stream, gain_first, shift_first = norm_pullback(grad_normed)
-        upstream = grad_stream + grad_middle
-        gradients = (
-            jnp.stack([gain_first, gain_second]),
-            jnp.stack([shift_first, shift_second]),
-            heads_grad,
-            offsets_grad,
-            merge_grad,
-            jnp.stack([bias_first, bias_second]),
-            expand_grad,
-            hidden_grad,
-            shrink_grad,
-        )
-        layer_grads[layer_index] = gradients
-    stacked = reduce_grads(layer_grads)
+    weights = dict(shrink=shrink_weight, expand=expand_weight, merge=merge_weight, heads=heads_weight)
+    flat, grad_tokens, small = backward(
+        kept, weights, norm_gain[:, :, None], jnp.stack(lses), positions[None], cotangent
+    )
+    ranks = lax.axis_size("dp")
+    if ranks > BLOCK:
+        groups = [[j * BLOCK + i for j in range(ranks // BLOCK)] for i in range(BLOCK)]
+        flat, small = lax.psum((flat, small), "dp", axis_index_groups=groups)
+    width = tokens.shape[1]
+    flat = flat.reshape(LAYERS, PER_LAYER, 2, UNIT, UNIT)[::-1]
+    small = small.reshape(LAYERS, SMALL, width)
+    shrink = flat[:, 0:4].reshape(LAYERS, 2, 2, 2, UNIT, UNIT).transpose(0, 1, 3, 4, 2, 5).reshape(shrink_weight.shape)
+    expand = flat[:, 4:8].transpose(0, 2, 3, 1, 4).reshape(expand_weight.shape)
+    merge = flat[:, 8].transpose(0, 2, 1, 3).reshape(merge_weight.shape)
+    heads = flat[:, 9:12].reshape(heads_weight.shape)
     return (
         output,
-        upstream.astype(jnp.bfloat16),
-        stacked[0],
-        stacked[1],
-        stacked[2],
-        stacked[3],
-        stacked[4],
-        stacked[5],
-        stacked[6],
-        stacked[7],
-        stacked[8],
+        grad_tokens,
+        small[:, GAIN : GAIN + 2],
+        small[:, SHIFT : SHIFT + 2],
+        heads,
+        small[:, OFFSETS].reshape(offsets.shape),
+        merge,
+        small[:, BRANCH : BRANCH + 2],
+        expand,
+        small[:, HIDDEN : HIDDEN + 2].reshape(hidden_bias.shape),
+        shrink,
     )
 
 

time: 1160 us -> 745 us (0.64)
  matrix products: 236 us -> 60.1 us
  local copies, waits for them, and re-layouts: 220 us -> 143 us
  blocking collectives: 75.1 us -> 0 us
  other arithmetic: 119 us -> 50.7 us
  waiting for transfers between devices: 97 us -> 66.6 us
  Pallas kernels: 378 us -> 402 us
    dot_general x32 -> x0, matrix products: 165 us -> none  [the longest x4 22.9 us: one_block(): jnp.einsum('hqk,khd->qhd', grad_scores, key_rows, preferred_element_type=...]
    psum x1 -> x0, blocking collectives: 75.1 us -> none  [reduce_grads(): small = lax.psum(small, 'dp')]
    transpose x12 -> x2, local copies, waits for them, and re-layouts: 63.4 us -> 17.8 us  [on_device(): expand = flat[:, 4:8].transpose(0, 2, 3, 1, 4).reshape(expand_weight.shape)]
    another operation x28 -> x7, local copies, waits for them, and re-layouts: 34.3 us -> 0.75 us  [the longest x1 0.61 us: on_device(): small[:, OFFSETS].reshape(offsets.shape)]
    slice x3 -> x8, local copies, waits for them, and re-layouts: 4.28 us -> 34.7 us  [the longest x2 19.2 us: on_device(): flat[:, 0:4].reshape(LAYERS, 2, 2, 2, UNIT, UNIT)]
    reduce_sum x12 -> x0, other arithmetic: 24.6 us -> none  [the longest x5 17 us: layer_norm(): return centre * lax.rsqrt(spread + 1e-05) * gain_row + shift_row]
    psum x3 -> x0, waiting for transfers between devices: 24.5 us -> none  [reduce_inputs(): return lax.psum(partial_sum, 'tensor')]
    pallas_call x1, Pallas kernels: 378 us -> 402 us  [backward(): pl.pallas_call(kernel, out_shape=(flat, flat, jax.ShapeDtypeStruct((T, D)...]
  transfers between devices with their start and end apart: 7 -> 4, of which waited for: 4 -> 3; matrix products, arithmetic and copies ran while one was open for 21% -> 16% of each run, Pallas kernels for 33% -> 54%
where the time goes in v2:
time: 745 us; the launch traced here: 740 us
  Pallas kernels  402 us (54%)
  local copies, waits for them, and re-layouts  143 us (19%)
  waiting for transfers between devices  66.6 us (9%)
  matrix products  60.1 us (8%)
  other arithmetic  50.7 us (7%)
  between operations  14.7 us (2%)
    pallas_call x1, Pallas kernels, backward(): pl.pallas_call(kernel, out_shape=(flat, flat, jax.ShapeDtypeStruct((T, D)...  402 us
    psum x4, waiting for transfers between devices, add_branch(): return stream + (lax.psum(partial_sum, 'tensor') + bias_row)  66.6 us
    reshape x2, local copies, waits for them, and re-layouts, on_device(): flat[:, 0:4].reshape(LAYERS, 2, 2, 2, UNIT, UNIT)  30.3 us
    slice x2, local copies, waits for them, and re-layouts, on_device(): flat[:, 0:4].reshape(LAYERS, 2, 2, 2, UNIT, UNIT)  19.2 us
    transpose x2, local copies, waits for them, and re-layouts, on_device(): expand = flat[:, 4:8].transpose(0, 2, 3, 1, 4).reshape(expand_weight.shape)  17.8 us
    dot_general x4, matrix products, one_block(): jnp.einsum('hqk,khd->qhd', chances, value_rows, preferred_element_type=jn...  17.7 us
    unnamed x112, local copies, waits for them, and re-layouts  15.2 us
  transfers between devices with their start and end apart: 4, of which 3 were waited for; matrix products, arithmetic and copies ran while one was open for 16% of the time, Pallas kernels for 54%

profile of v2, /device:TPU:0, one launch (start us, length us, event | category | flops | bytes accessed | tf_op | source)
XLA Modules:
  0.0 739.8 jit_solution(17747560144375087205)
XLA Ops:
  9.1 2.1 multiply_reduce_fusion.3
  13.7 2.2 convolution_bitcast_fusion.1
  23.2 1.9 copy.42
  27.7 24.8 %while.42 = (s32[]{:T(128)}, bf16[2,512,6,64]{1,3,2,0:T(8,128)(2,1)S(1)}, f32[2,6,512]{2,1,0:T(8,128)S(1)}, s32[2]{0:T(128)S(1)}, s32[2,512]{1,0:T(2,128)S(1)}, ...) while((s32[]{:T(128)}, ...), condition=%wide.region_5.6_spmd, body=%wide.region_2.5_spmd.sunk | while | flops 844822528 | bytes 45484204 | solution.py:781
  29.6 2.4 fusion.95
  32.0 3.6 fusion.96
  35.7 4.4 fusion.97
  42.0 2.4 fusion.95
  44.4 3.6 fusion.96
  48.1 4.4 fusion.97
  54.5 2.7 fusion.60
  58.5 24.7 %all-reduce.7.cloned.1.call-done = f32[1024,768]{1,0:T(8,128)} async-done(((f32[1024,768]{1,0:T(8,128)}), f32[1024,768]{1,0:T(8,128)}) %all-reduce.7.cloned.1.call-update) | async-done | bytes 3145744 | tf_op jit(solution)/shard_map/psum | solution.py:793
  83.2 3.0 fusion.66
  87.8 5.9 fusion.32
  95.4 4.3 fusion.41
  100.4 23.8 %all-reduce.9.cloned.1.call-done = f32[1024,768]{1,0:T(8,128)} async-done(((f32[1024,768]{1,0:T(8,128)}), f32[1024,768]{1,0:T(8,128)}) %all-reduce.9.cloned.1.call-update) | async-done | bytes 3145744 | tf_op jit(solution)/shard_map/psum | solution.py:793
  124.2 2.3 fusion.65
  129.7 2.2 convolution_bitcast_fusion
  138.4 1.9 copy.49
  142.8 24.8 %while.43 = (s32[]{:T(128)}, bf16[2,512,6,64]{1,3,2,0:T(8,128)(2,1)S(1)}, f32[2,6,512]{2,1,0:T(8,128)S(1)}, s32[2]{0:T(128)S(1)}, s32[2,512]{1,0:T(2,128)S(1)}, ...) while((s32[]{:T(128)}, ...), condition=%wide.region_15.16_spmd, body=%wide.region_12.15_spmd.sunk | while | flops 844822528 | bytes 45484204 | solution.py:781
  144.7 2.4 fusion.101
  147.1 3.6 fusion.102
  150.7 4.4 fusion.103
  157.1 2.4 fusion.101
  159.5 3.6 fusion.102
  163.2 4.4 fusion.103
  169.5 2.7 fusion.58
  172.3 2.5 copy.52.refs_2_
  174.8 3.3 convert_element_type.79.refs_3_
  178.7 18.1 %all-reduce.11.cloned.1.call-done = f32[1024,768]{1,0:T(8,128)} async-done(((f32[1024,768]{1,0:T(8,128)}), f32[1024,768]{1,0:T(8,128)}) %all-reduce.11.cloned.1.call-update) | async-done | bytes 3145744 | tf_op jit(solution)/shard_map/psum | solution.py:793
  196.7 2.3 fusion.64
  200.7 8.5 %fusion.37 = (bf16[1024,1536]{1,0:T(8,128)(2,1)S(1)}, f32[1024,1536]{1,0:T(8,128)}) fusion(f32[1536]{0:T(1024)S(1)} %copy-done.47, bf16[1024,768]{1,0:T(8,128)(2,1)S(1)} %add_convert_fusion.1.refs_17_, bf16[2,768,1536]{2,1,0:T(8,128)(2,1)} %refs_21_.1), kind=kOutput, calls=%fused_computation.57 | convolution fusion | flops 2431647744 | bytes 13375488 | tf_op jit(solution)/shard_map/dot_general | solution.py:849
  211.0 4.3 fusion.38
  215.4 2.5 slice_bitcast_fusion.1.refs_5_
  217.9 3.3 fusion.54
  222.9 2.4 slice_bitcast_fusion.2.refs_15_
  225.4 3.5 fusion.52
  228.9 401.9 %shard_map.203 = (f32[24,2,384,384]{3,2,1,0:T(8,128)}, f32[24,2,384,384]{3,2,1,0:T(8,128)}, bf16[1024,768]{1,0:T(8,128)(2,1)}, f32[32,768]{1,0:T(8,128)}) custom-call(bf16[1024,768]{1,0:T(8,128)(2,1)} %refs_0_.1, bf16[1024,1536]{1,0:T(8,128)(2,1)} %copy-done.19, bf16[1024,384]{1,0:T(8,128)(2,1)} %copy.52.refs_2_, f32[1024,768]{1,0:T(8,128)} %convert_element_type.79.refs_3_, ...), custom_call_target="tpu_custom_call" | custom-call | tf_op jit(solution)/shard_map/pallas_call | solution.py:718
  630.8 6.3 slice.188
  639.0 11.0 %fusion.67 = (f32[2,4,2,384,384]{4,3,2,1,0:T(8,128)}, f32[2,4,2,384,384]{4,3,2,1,0:T(8,128)S(1)}) fusion(f32[2,12,2,384,384]{4,3,2,1,0:T(8,128)} %bitcast.181), kind=kLoop, calls=%fused_computation.146 | loop fusion | bytes 37748736 | tf_op jit(solution)/shard_map/slice | solution.py:876
  649.9 4.4 reverse_bitcast_fusion
  654.4 13.4 %copy.55 = f32[2,2,384,4,384]{4,3,2,1,0:T(4,128)} copy(f32[2,2,384,4,384]{4,2,1,3,0:T(8,128)} %reverse_bitcast_fusion) | data formatting | bytes 18874368 | tf_op jit(solution)/shard_map/transpose | solution.py:877
  667.7 12.0 %reshape.352 = f32[2,768,1536]{2,1,0:T(8,128)} reshape(f32[2,2,384,4,384]{4,3,2,1,0:T(4,128)} %copy.55) | data formatting | bytes 18874368 | tf_op jit(solution)/shard_map/reshape | solution.py:877
  679.8 8.2 %slice.179 = f32[2,4,2,384,384]{4,3,2,1,0:T(8,128)} reverse(f32[2,4,2,384,384]{4,3,2,1,0:T(8,128)} %get-tuple-element.245), dimensions={0} | reverse | bytes 18874368 | tf_op jit(solution)/shard_map/slice | solution.py:876
  688.0 17.3 %copy.66 = f32[2,2,2,2,384,384]{5,2,4,3,1,0:T(2,128)} copy(f32[2,2,2,2,384,384]{5,4,3,2,1,0:T(8,128)} %bitcast.175) | data formatting | bytes 18874368 | tf_op jit(solution)/shard_map/reshape | solution.py:876
  705.3 13.0 %reshape.355 = f32[2,1536,768]{2,1,0:T(8,128)} reshape(f32[2,2,2,384,2,384]{5,4,3,2,1,0:T(2,128)} %bitcast.176) | data formatting | bytes 18874368 | tf_op jit(solution)/shard_map/reshape | solution.py:876
  718.3 6.4 slice.170
  728.4 3.6 add_convert_fusion
  (210 shorter events, 52.5 us)
Async XLA Ops:
  7.2 4.7 copy-start.5
  7.2 4.1 copy-start.26
  7.2 4.0 copy-start.44
  7.2 76.0 %all-reduce.7.cloned.1.call-start = ((), (), s32[]{:S(2)}) async-start(), calls=%async_computation | async-start | bytes 6291456 | tf_op jit(solution)/shard_map/psum | solution.py:793
  7.3 6.4 copy-start.17
  15.9 2.7 copy-start.6
  19.5 1.8 copy-start.48
  22.0 3.1 copy-start.33
  23.1 3.5 copy-start.43
  32.0 3.7 copy-start.23
  44.4 3.7 copy-start.23
  52.6 4.6 copy-start.24
  52.6 1.9 copy-start.15
  54.5 2.8 copy-start.45
  54.5 3.4 copy-start.46
  57.2 67.1 %all-reduce.9.cloned.1.call-start = ((), (), s32[]{:S(2)}) async-start(), calls=%async_computation.1 | async-start | bytes 6291456 | tf_op jit(solution)/shard_map/psum | solution.py:793
  83.2 4.1 slice-start
  86.2 38.0 %copy-start = (f32[1024,768]{1,0:T(8,128)}, f32[1024,768]{1,0:T(8,128)S(1)}, u32[]{:S(2)}) copy-start(f32[1024,768]{1,0:T(8,128)S(1)} %get-tuple-element.236.refs_4_) | copy-start | bytes 9437188
  86.2 9.1 %slice-start.2 = ((s8[4718592]{0:T(1024)(128)(4,1)}), s8[4194304]{0:T(1024)(128)(4,1)S(1)}, s32[]{:S(2)}) async-start(s8[4718592]{0:T(1024)(128)(4,1)} %bitcast.191), calls=%async_computation.6 | async-start | bytes 8388608
  87.3 6.4 copy-start.12
  87.8 7.5 %slice-start.3 = ((s8[4718592]{0:T(1024)(128)(4,1)}), s8[524288]{0:T(1024)(128)(4,1)S(1)}, s32[]{:S(2)}) async-start(s8[4718592]{0:T(1024)(128)(4,1)} %bitcast.191), calls=%async_computation.7 | async-start | bytes 1048576
  93.7 1.6 copy-start.19
  99.7 97.1 %all-reduce.11.cloned.1.call-start = ((), (), s32[]{:S(2)}) async-start(), calls=%async_computation.2 | async-start | bytes 6291456 | tf_op jit(solution)/shard_map/psum | solution.py:793
  127.1 2.6 copy-start.18
  129.7 2.2 copy-start.13
  131.9 2.6 copy-start.7
  147.1 3.7 copy-start.22
  159.5 3.7 copy-start.22
  167.6 1.9 copy-start.16
  172.2 5.9 copy-start.27
  172.2 6.5 copy-start.25
  172.2 24.5 %copy-start.4 = (f32[1024,768]{1,0:T(8,128)S(1)}, f32[1024,768]{1,0:T(8,128)}, u32[]{:S(2)}) copy-start(f32[1024,768]{1,0:T(8,128)} %copy-done.3) | copy-start | bytes 9437188
  172.2 24.5 %copy-start.42 = (f32[768]{0:T(1024)S(1)}, f32[768]{0:T(1024)}, u32[]{:S(2)}) copy-start(f32[768]{0:T(1024)} %get-tuple-element.184) | copy-start | bytes 9220
  172.2 556.1 %all-reduce.13.cloned.1.call-start = ((), (), s32[]{:S(2)}) async-start(), calls=%async_computation.3 | async-start | bytes 6291456 | tf_op jit(solution)/shard_map/psum | solution.py:793
  199.1 1.7 copy-start.1
  199.1 11.9 %slice-start.4 = ((s8[4718592]{0:T(1024)(128)(4,1)}), s8[524288]{0:T(1024)(128)(4,1)S(1)}, s32[]{:S(2)}) async-start(s8[4718592]{0:T(1024)(128)(4,1)} %bitcast.193), calls=%async_computation.8 | async-start | bytes 1048576
  200.7 8.5 %copy-start.14 = (bf16[1024,768]{1,0:T(8,128)(2,1)}, bf16[1024,768]{1,0:T(8,128)(2,1)S(1)}, u32[]{:S(2)}) copy-start(bf16[1024,768]{1,0:T(8,128)(2,1)S(1)} %add_convert_fusion.1.refs_17_) | copy-start | bytes 4718596
  200.7 10.3 %slice-start.5 = ((s8[4718592]{0:T(1024)(128)(4,1)}), s8[4194304]{0:T(1024)(128)(4,1)S(1)}, s32[]{:S(2)}) async-start(s8[4718592]{0:T(1024)(128)(4,1)} %bitcast.193), calls=%async_computation.9 | async-start | bytes 8388608
  209.2 1.8 copy-start.20
  215.4 2.5 copy-start.34
  215.4 2.5 copy-start.36
  215.4 5.8 copy-start.10
  217.9 7.5 %copy-start.30 = (f32[384]{0:T(512)S(1)}, f32[384]{0:T(512)}, u32[]{:S(2)}) copy-start(f32[384]{0:T(512)} %get-tuple-element.195) | copy-start | bytes 4612
  217.9 7.5 %copy-start.32 = (f32[384]{0:T(512)S(1)}, f32[384]{0:T(512)}, u32[]{:S(2)}) copy-start(f32[384]{0:T(512)} %get-tuple-element.198) | copy-start | bytes 4612
  724.9 1.6 copy-start.28
  724.9 3.5 copy-start.2
  724.9 3.5 copy-start.37
  728.4 3.6 copy-start.21
  (13 other events, 12.8 us)
Sparse Core Ops, SparseCore 0:
  57.3 25.8 all-reduce.6
  99.8 24.3 all-reduce.8
  172.3 24.3 all-reduce.10
  215.5 24.3 all-reduce.12

commit v3 on v2

v3 whole, which is shorter than its diff:
```python
from types import SimpleNamespace

import jax
import jax.numpy as jnp
from jax import lax
from jax.experimental import pallas as pl
from jax.experimental.pallas import tpu as pltpu
from jax.sharding import PartitionSpec as P

LAYERS = 2
UNIT = 384
BLOCK = 16
MESH = pl.DeviceIdType.MESH


class Exchange:
    def __init__(self, groups, rows, cols, slots, lags):
        self.groups, self.rows, self.cols, self.slots = groups, rows, cols, slots
        self.half = rows // 2
        self.chunk = self.half // 4
        starts = [0]
        for lag in lags:
            starts.append(starts[-1] + lag)
        self.starts = starts
        self.ticks = groups + starts[-1]
        self.last_slots = starts[9]
        self.gather_slots = max(starts[8] - starts[1], slots)

    def scratch(self):
        groups, slots, half, chunk, cols = self.groups, self.slots, self.half, self.chunk, self.cols
        dma = pltpu.SemaphoreType.DMA
        plain = pltpu.SemaphoreType.REGULAR
        return dict(
            held=pltpu.VMEM((self.held_slots(), 2, half, cols), jnp.float32),
            swap_in=pltpu.VMEM((slots, 2, half, cols), jnp.float32),
            chain_in=pltpu.VMEM((slots, 3, 2, 2, chunk, cols), jnp.float32),
            third_in=pltpu.VMEM((slots, 2, chunk, cols), jnp.float32),
            swap_s=dma((slots,)), swap_r=dma((slots,)),
            chain_s=dma((slots, 3, 2)), chain_r=dma((slots, 3, 2)),
            third_s=dma((slots,)), third_r=dma((slots,)),
            gather_s=dma((slots, 3, 2)), gather_r=dma((self.gather_slots, 3, 2)),
            last_s=dma((slots,)), last_r=dma((self.last_slots,)),
            own_s=dma((slots,)), load_s=dma((slots,)),
            swap_c=plain((2,)), chain_c=plain((3, 2)), third_c=plain((2,)),
        )

    def held_slots(self):
        return self.groups

    def setup(self, refs):
        self.refs = refs
        dp = lax.axis_index("dp")
        core = lax.axis_index("tensor")
        low = lax.rem(dp, 16)
        self.dp, self.core = dp, core
        self.z = lax.div(low, 4)
        self.y = lax.rem(lax.div(low, 2), 2)
        self.x = lax.rem(low, 2)
        self.step_x = 1 - 2 * self.x
        self.step_y = 2 - 4 * self.y
        self.along = ((dp + 4, core), (dp - 4, core))

    def barrier(self, others=()):
        z = self.z
        bar = pltpu.get_barrier_semaphore()

        def greet(device):
            pl.semaphore_signal(bar, inc=1, device_id=device, device_id_type=MESH)

        for device in ((self.dp + self.step_x, self.core), (self.dp + self.step_y, self.core)) + tuple(others):
            greet(device)

        @pl.when(z < 3)
        def _():
            greet(self.along[0])

        @pl.when(z > 0)
        def _():
            greet(self.along[1])

        pl.semaphore_wait(bar, 2 + len(others) + (z < 3).astype(jnp.int32) + (z > 0).astype(jnp.int32))

    def first(self, g):
        return (self.dp + jnp.where(lax.rem(g, 2) == 0, self.step_x, self.step_y), self.core)

    def third(self, g):
        return (self.dp + jnp.where(lax.rem(g, 2) == 0, self.step_y, self.step_x), self.core)

    def side(self, g):
        return jnp.where(lax.rem(g, 2) == 0, self.x, self.y)

    def copy(self, src, dst, send, recv, device):
        return pltpu.make_async_remote_copy(
            src_ref=src, dst_ref=dst, send_sem=send, recv_sem=recv, device_id=device, device_id_type=MESH
        )

    def rows_of(self, j):
        return pl.ds(pl.multiple_of(j * self.chunk, 8), self.chunk)

    def held(self, g):
        return self.refs.held.at[g]

    def swap(self, g):
        r, k = self.refs, lax.rem(g, self.slots)
        return self.copy(self.sent_half(g), r.swap_in.at[k], r.swap_s.at[k], r.swap_r.at[k], self.first(g))

    def chain_send(self, step, d, g):
        z, r, k = self.z, self.refs, lax.rem(g, self.slots)
        j = 4 - step + z if d == 0 else step - 4 + z
        here = ((z < 3) & (step > z)) if d == 0 else ((z > 0) & (step > 3 - z))
        at = (k, step - 1, d)
        part = self.held(g).at[:, self.rows_of(j)]
        return here, self.copy(part, r.chain_in.at[at], r.chain_s.at[at], r.chain_r.at[at], self.along[d])

    def start_chain(self, step, g):
        for d in range(2):
            here, copy = self.chain_send(step, d, g)

            @pl.when(here)
            def _():
                @pl.when(g >= self.slots)
                def _():
                    pl.semaphore_wait(self.refs.chain_c.at[step - 1, d], 1)

                copy.start()

    def finish_chain(self, step, g):
        z, r, k = self.z, self.refs, lax.rem(g, self.slots)
        for d in range(2):
            here, copy = self.chain_send(step, d, g)

            @pl.when(here)
            def _():
                copy.wait_send()

        for d in range(2):
            here = ((z >= 1) & (step >= z)) if d == 0 else ((z <= 2) & (step >= 3 - z))
            j = 3 - step + z if d == 0 else step - 3 + z
            at = (k, step - 1, d)

            @pl.when(here)
            def _():
                came = r.chain_in.at[at]
                self.copy(came, came, r.chain_s.at[at], r.chain_r.at[at], self.along[1 - d]).wait_recv()
                part = self.held(g).at[:, self.rows_of(j)]
                part[...] = part[...] + came[...]

                @pl.when(g + self.slots < self.groups)
                def _():
                    pl.semaphore_signal(
                        r.chain_c.at[step - 1, d], inc=1, device_id=self.along[1 - d], device_id_type=MESH
                    )

    def third_swap(self, g):
        r, k = self.refs, lax.rem(g, self.slots)
        part = self.held(g).at[:, self.rows_of(self.z)]
        return self.copy(part, r.third_in.at[k], r.third_s.at[k], r.third_r.at[k], self.third(g))

    def gather_copy(self, step, d, g, j, source=None):
        r, k = self.refs, lax.rem(g, self.slots)
        part = self.result(g, self.side(g) * self.half + j * self.chunk, self.chunk)
        return self.copy(
            part if source is None else source,
            part,
            r.gather_s.at[k, step - 1, d],
            r.gather_r.at[lax.rem(g, self.gather_slots), step - 1, d],
            self.along[d],
        )

    def gather_send(self, step, d, g):
        z = self.z
        j = z - (step - 1) if d == 0 else z + step - 1
        here = ((z < 3) & (step - 1 <= z)) if d == 0 else ((z > 0) & (z + step - 1 <= 3))
        source = self.held(g).at[:, self.rows_of(z)] if step == 1 else None
        return here, self.gather_copy(step, d, g, j, source)

    def start_gather(self, step, g):
        for d in range(2):
            here, copy = self.gather_send(step, d, g)

            @pl.when(here)
            def _():
                copy.start()

    def finish_gather(self, step, g):
        z = self.z
        for d in range(2):
            here, copy = self.gather_send(step, d, g)

            @pl.when(here)
            def _():
                copy.wait_send()

        for d in range(2):
            here = (z >= step) if d == 0 else (z + step <= 3)
            j = z - step if d == 0 else z + step

            @pl.when(here)
            def _():
                self.gather_copy(step, d, g, j).wait_recv()

    def own_copy(self, g):
        k = lax.rem(g, self.slots)
        part = self.held(g).at[:, self.rows_of(self.z)]
        return pltpu.make_async_copy(
            part, self.result(g, self.side(g) * self.half + self.z * self.chunk, self.chunk), self.refs.own_s.at[k]
        )

    def last(self, g):
        r, k = self.refs, lax.rem(g, self.slots)
        part = self.result(g, self.side(g) * self.half, self.half)
        return self.copy(part, part, r.last_s.at[k], r.last_r.at[lax.rem(g, self.last_slots)], self.first(g))

    def stage(self, e, g):
        r, slots, groups = self.refs, self.slots, self.groups
        k = lax.rem(g, slots)
        if e == 0:
            self.prepare(g)

            @pl.when(g >= slots)
            def _():
                pl.semaphore_wait(r.swap_c.at[lax.rem(g, 2)], 1)

            self.swap(g).start()
        elif e == 1:
            self.settle(g)
            copy = self.swap(g)
            copy.wait_send()
            copy.wait_recv()
            mine = self.held(g)
            mine[...] = mine[...] + r.swap_in[k]

            @pl.when(g + slots < groups)
            def _():
                pl.semaphore_signal(
                    r.swap_c.at[lax.rem(g, 2)], inc=1, device_id=self.first(g), device_id_type=MESH
                )

            self.start_chain(1, g)
        elif e in (2, 3):
            self.finish_chain(e - 1, g)
            self.start_chain(e, g)
        elif e == 4:
            self.finish_chain(3, g)

            @pl.when(g >= slots)
            def _():
                pl.semaphore_wait(r.third_c.at[lax.rem(g, 2)], 1)

            self.third_swap(g).start()
        elif e == 5:
            copy = self.third_swap(g)
            copy.wait_send()
            copy.wait_recv()
            part = self.held(g).at[:, self.rows_of(self.z)]
            part[...] = part[...] + r.third_in[k]

            @pl.when(g + slots < groups)
            def _():
                pl.semaphore_signal(
                    r.third_c.at[lax.rem(g, 2)], inc=1, device_id=self.third(g), device_id_type=MESH
                )

            self.start_gather(1, g)
            self.own_copy(g).start()
        elif e in (6, 7):
            self.finish_gather(e - 5, g)
            if e == 6:
                self.own_copy(g).wait()
            self.start_gather(e - 4, g)
        elif e == 8:
            self.finish_gather(3, g)
            self.last(g).start()
        else:
            copy = self.last(g)
            copy.wait_send()
            copy.wait_recv()

    def tick(self, t):
        for e in reversed(range(10)):
            g = t - self.starts[e]

            @pl.when((g >= 0) & (g < self.groups))
            def _():
                self.stage(e, g)


class FlatExchange(Exchange):
    def part(self, whole, g, start, size):
        start = lax.rem(g, 2) * self.rows + start
        return whole.at[lax.div(g, 2), :, pl.ds(pl.multiple_of(start, 8), size)]

    def sent_half(self, g):
        return self.part(self.source, g, (1 - self.side(g)) * self.half, self.half)

    def load(self, g):
        k = lax.rem(g, self.slots)
        own = self.part(self.source, g, self.side(g) * self.half, self.half)
        return pltpu.make_async_copy(own, self.held(g), self.refs.load_s.at[k])

    def prepare(self, g):
        self.load(g).start()

    def settle(self, g):
        self.load(g).wait()

    def result(self, g, start, size):
        return self.part(self.target, g, start, size)


ROWS = 256


def dot(a, b, dims):
    return lax.dot_general(a, b, (dims, ((), ())), preferred_element_type=jnp.float32)


NN = ((1,), (0,))
NT = ((1,), (1,))
TN = ((0,), (0,))


def gelu_slope(x):
    t = jnp.tanh(0.7978845608028654 * (x + 0.044715 * x * x * x))
    return 0.5 * (1.0 + t) + 0.5 * x * (1.0 - t * t) * (
        0.7978845608028654 * (1.0 + 3.0 * 0.044715 * x * x)
    )


def norm_parts(h):
    centre = h - jnp.mean(h, axis=-1, keepdims=True)
    r = lax.rsqrt(jnp.mean(centre * centre, axis=-1, keepdims=True) + 1e-05)
    return centre * r, r


GAIN, SHIFT, BRANCH, HIDDEN, OFFSETS, SMALL = 0, 2, 4, 6, 8, 16
PIECES = 21
ATTEND = range(11, 17)
LATE = {1: ((1, 1),), 2: ((0, 2),), 3: ((1, 3),), 7: ((1, 5),), 8: ((0, 6), (1, 7)), 10: ((0, 8),)}
PER_LAYER = 12


ACT, PRE, NORM, H, ATT, Q, K, V = "act", "pre", "norm", "h", "att", "q", "k", "v"
W_SHRINK, W_EXPAND, W_MERGE, W_HEADS = "w_shrink", "w_expand", "w_merge", "w_heads"
NORM1, NORM2, H_MID = "norm1", "norm2", "h_mid"
SHRINK, EXPAND, MERGE, HEADS = "shrink", "expand", "merge", "heads"


class Backward(FlatExchange):
    LOADS = (ACT, PRE, NORM, H, ATT, Q, K, V, W_SHRINK, W_EXPAND, W_MERGE, W_HEADS)

    def more_scratch(self):
        T, D, W, F = self.T, self.D, self.W, self.F
        low, full = jnp.bfloat16, jnp.float32
        dma = pltpu.SemaphoreType.DMA
        return dict(
            act=pltpu.VMEM((T, F), low), pre=pltpu.VMEM((T, F), full), norm=pltpu.VMEM((T, D), low),
            h=pltpu.VMEM((T, D), full), att=pltpu.VMEM((T, W), low), q=pltpu.VMEM((T, W), low),
            k=pltpu.VMEM((T, W), low), v=pltpu.VMEM((T, W), low), w_shrink=pltpu.VMEM((F, D), low),
            w_expand=pltpu.VMEM((D, F), low), w_merge=pltpu.VMEM((W, D), low), w_heads=pltpu.VMEM((3, D, W), low),
            g=pltpu.VMEM((T, D), full), low=pltpu.VMEM((T, D), low), came=pltpu.VMEM((T, D), full),
            datt=pltpu.VMEM((T, W), low), dqkv=pltpu.VMEM((3, T, W), low),
            staged=pltpu.VMEM((2, 2, 384, 384), full), dk=pltpu.VMEM((T, 128), full), dv=pltpu.VMEM((T, 128), full),
            small=pltpu.VMEM((2 * SMALL, D), full), small_in=pltpu.VMEM((4, 2 * SMALL, D), full),
            input_s=dma((len(self.LOADS),)), cot_s=dma, staged_s=dma((2,)), tokens_s=dma,
            core_s=dma((T // ROWS,)), core_r=dma((T // ROWS,)), core_c=pltpu.SemaphoreType.REGULAR,
            small_s=dma((4,)), small_r=dma((4,)),
        )

    def held_slots(self):
        return self.starts[6]

    def held(self, g):
        return self.refs.held.at[lax.rem(g, self.held_slots())]

    def fetch(self, name, layer, second=False):
        source = self.inputs[name][layer]
        if name in (NORM, H):
            source = source[1 if second else 0]
        pltpu.make_async_copy(source, getattr(self.refs, name), self.refs.input_s.at[self.LOADS.index(name)]).start()

    def arrive(self, name):
        source = self.inputs[name][0]
        if name in (NORM, H):
            source = source[0]
        pltpu.make_async_copy(source, getattr(self.refs, name), self.refs.input_s.at[self.LOADS.index(name)]).wait()

    def fetch_next(self, l, *names, second=False):
        @pl.when(l == 1)
        def _():
            for name in names:
                self.fetch(name, 0, second)

    def stage_copy(self, at, g):
        return pltpu.make_async_copy(self.refs.staged.at[at], self.source.at[g], self.refs.staged_s.at[at])

    def core_copy(self, i):
        r = self.refs
        rows = pl.ds(pl.multiple_of(i * ROWS, ROWS), ROWS)
        return self.copy(
            r.pre.at[rows, pl.ds(0, self.D)], r.came.at[rows], r.core_s.at[i], r.core_r.at[i],
            (self.dp, 1 - self.core),
        )

    def partial(self, make, wait):
        @pl.when(wait)
        def _():
            pl.semaphore_wait(self.refs.core_c, 1)

        def block(i, carry):
            rows = pl.ds(pl.multiple_of(i * ROWS, ROWS), ROWS)
            self.refs.pre[rows, 0 : self.D] = make(rows)
            self.core_copy(i).start()
            return carry

        lax.fori_loop(0, self.T // ROWS, block, 0)

    def norm_back(self, l, which, more, after):
        r, D = self.refs, self.D
        gain = self.gain[l, which : which + 1]
        n = 128
        blocks = ROWS // n

        def block(i, carry):
            @pl.when(lax.rem(i, blocks) == 0)
            def _():
                copy = self.core_copy(lax.div(i, blocks))
                copy.wait_send()
                copy.wait_recv()

            rows = pl.ds(pl.multiple_of(i * n, n), n)
            xhat, rstd = norm_parts(r.h[rows])
            d = r.pre[rows, 0:D] + r.came[rows]
            e = d * gain
            spread = xhat * jnp.mean(e * xhat, axis=-1, keepdims=True)
            new = r.g[rows] + rstd * (e - jnp.mean(e, axis=-1, keepdims=True) - spread)
            r.g[rows] = new
            rounded = new.astype(jnp.bfloat16)
            r.low[rows] = rounded
            return (
                carry[0] + jnp.sum(d * xhat, axis=0, keepdims=True),
                carry[1] + jnp.sum(d, axis=0, keepdims=True),
                carry[2] + jnp.sum(rounded.astype(jnp.float32), axis=0, keepdims=True),
            )

        zero = jnp.zeros((1, D), jnp.float32)
        sums = lax.fori_loop(0, self.T // n, block, (zero, zero, zero))
        self.row(l, GAIN + which)[...] = sums[0]
        self.row(l, SHIFT + which)[...] = sums[1]
        after(sums[2])

        @pl.when(more)
        def _():
            pl.semaphore_signal(
                r.core_c, inc=1, device_id=(self.dp, 1 - self.core), device_id_type=MESH
            )

    def row(self, l, at, start=0, size=None):
        size = self.D if size is None else size
        return self.refs.small.at[pl.ds(l * SMALL + at, 1), start : start + size]

    def outer(self, left, left_at, right, right_at, at, job):
        for u in range(2):
            a = left[:, pl.ds(pl.multiple_of(left_at + u * UNIT, 128), UNIT)]
            self.refs.staged[at, u] = dot(a, right[:, right_at * UNIT : (right_at + 1) * UNIT], TN)
        self.stage_copy(at, job).start()

    def shrink_job(self, i, job):
        self.outer(self.refs.act, i // 2 * 2 * UNIT, self.refs.low, i % 2, i % 2, job)

    def expand_job(self, i, job):
        self.outer(self.refs.norm, 0, self.refs.act, i, i % 2, job)

    def slopes(self, first, last, l):
        r, F, D = self.refs, self.F, self.D

        def one(i, carry):
            rows = pl.ds(pl.multiple_of(i * ROWS, ROWS), ROWS)
            sums = []
            for c in range(0, F, 512):
                d_act = dot(r.low[rows], r.w_shrink[c : c + 512], NT)
                d_pre = (d_act * gelu_slope(r.pre[rows, c : c + 512])).astype(jnp.bfloat16)
                r.act[rows, c : c + 512] = d_pre
                sums.append(carry[c // 512] + jnp.sum(d_pre.astype(jnp.float32), axis=0, keepdims=True))
            return tuple(sums)

        sums = lax.fori_loop(first, last, one, (jnp.zeros((1, 512), jnp.float32),) * (F // 512))
        for i, part in enumerate(sums):
            for j in range(2):
                at = i * 512 + j * 256
                row = self.row(l, HIDDEN + at // D, at % D, 256)
                row[...] = row[...] + part[:, j * 256 : (j + 1) * 256]

    def piece(self, p, l):
        r = self.refs
        T, W = self.T, self.W
        blocks = T // ROWS
        base = (1 - l) * PER_LAYER
        for q, job in LATE.get(p - 1, ()):
            self.stage_copy(q, base + job).wait()
        if p == 0:
            self.arrive(ACT)

            @pl.when(l == 1)
            def _():
                pltpu.make_async_copy(self.cotangent, r.low, r.cot_s).wait()
                for name in self.LOADS[1:]:
                    self.fetch(name, 1, second=True)

            self.shrink_job(0, base)
            self.stage_copy(0, base).wait()
        elif p in (1, 2, 3):
            self.shrink_job(p, base + p)
        elif p == 4:
            @pl.when(l == 1)
            def _():
                def widen(i, carry):
                    rows = pl.ds(pl.multiple_of(i * ROWS, ROWS), ROWS)
                    wide = r.low[rows].astype(jnp.float32)
                    r.g[rows] = wide
                    return carry + jnp.sum(wide, axis=0, keepdims=True)

                self.row(l, BRANCH + 1)[...] = lax.fori_loop(0, blocks, widen, jnp.zeros((1, self.D), jnp.float32))

            self.arrive(W_SHRINK)
            self.arrive(PRE)
            self.slopes(0, blocks // 2, l)
        elif p == 5:
            self.slopes(blocks // 2, blocks, l)
            self.fetch_next(l, W_SHRINK)
        elif p == 6:
            self.arrive(W_EXPAND)
            self.partial(lambda rows: dot(r.act[rows], r.w_expand[...], NT), l == 0)
        elif p == 7:
            self.arrive(NORM)
            self.expand_job(0, base + 4)
            self.expand_job(1, base + 5)
            self.stage_copy(0, base + 4).wait()
        elif p == 8:
            self.expand_job(2, base + 6)
            self.expand_job(3, base + 7)
            self.fetch_next(l, W_EXPAND, ACT)
            for layer in range(2):
                @pl.when(l == layer)
                def _():
                    self.fetch(NORM, layer)
        elif p == 9:
            self.arrive(H)

            def after(total):
                self.row(l, BRANCH)[...] = total

            self.norm_back(l, 1, jnp.bool_(True), after)
            for layer in range(2):
                @pl.when(l == layer)
                def _():
                    self.fetch(H, layer)
        elif p == 10:
            self.arrive(W_MERGE)
            self.arrive(ATT)

            def one(i, carry):
                rows = pl.ds(pl.multiple_of(i * ROWS, ROWS), ROWS)
                r.datt[rows] = dot(r.low[rows], r.w_merge[...], NT).astype(jnp.bfloat16)
                return carry

            lax.fori_loop(0, blocks, one, 0)
            for u in range(2):
                r.staged[0, u] = dot(r.att[...], r.low[:, u * UNIT : (u + 1) * UNIT], TN)
            self.stage_copy(0, base + 8).start()
        elif p in ATTEND:
            if p == ATTEND[0]:
                self.fetch_next(l, W_MERGE, ATT)
                self.arrive(Q)
                self.arrive(K)
                self.arrive(V)
            i = p - ATTEND[0]
            self.attend_back(i // 2, l, i % 2)
            if p == ATTEND[-1]:
                self.fetch_next(l, Q, K, V)
        elif p == 17:
            self.arrive(W_HEADS)

            def make(rows):
                total = dot(r.dqkv[0, rows], r.w_heads[0], NT)
                for c in (1, 2):
                    total = total + dot(r.dqkv[c, rows], r.w_heads[c], NT)
                return total

            self.partial(make, jnp.bool_(True))
            self.fetch_next(l, W_HEADS)
        elif p == 18:
            self.arrive(NORM)
            self.heads_job(0, base + 9)
            self.stage_copy(0, base + 9).wait()
        elif p == 19:
            self.heads_job(1, base + 10)
            self.heads_job(2, base + 11)
            for i, c in enumerate((0, 2)):
                self.row(l, OFFSETS, i * W, W)[...] = jnp.sum(r.dqkv[c].astype(jnp.float32), axis=0, keepdims=True)
            self.fetch_next(l, NORM, second=True)
            for c in (1, 2):
                self.stage_copy(c % 2, base + 9 + c).wait()
        else:
            self.arrive(H)

            def after(total):
                @pl.when(l == 1)
                def _():
                    self.row(0, BRANCH + 1)[...] = total

            self.norm_back(l, 0, l == 1, after)
            self.fetch_next(l, PRE)
            self.fetch_next(l, H, second=True)

            @pl.when(l == 0)
            def _():
                pltpu.make_async_copy(r.low, self.grad_tokens, r.tokens_s).start()

    def heads_job(self, c, job):
        r = self.refs
        for u in range(2):
            r.staged[c % 2, u] = dot(r.norm[:, u * UNIT : (u + 1) * UNIT], r.dqkv[c], TN)
        self.stage_copy(c % 2, job).start()

    def attend_back(self, pair, l, turn):
        r = self.refs
        T = self.T
        lanes = slice(pair * 128, (pair + 1) * 128)
        if turn == 0:
            r.dk[...] = jnp.zeros((T, 128), jnp.float32)
            r.dv[...] = jnp.zeros((T, 128), jnp.float32)
        lane = lax.broadcasted_iota(jnp.int32, (1, 128), 1)
        blocks = T // ROWS
        for b in range(blocks - 1) if turn == 0 else (blocks - 1,):
            rows, end = slice(b * ROWS, (b + 1) * ROWS), (b + 1) * ROWS
            query = b * ROWS + lax.broadcasted_iota(jnp.int32, (1, ROWS), 1)
            lowest = query - jnp.concatenate([self.positions[j : j + 1] for j in range(2 * b, 2 * b + 2)], axis=1)
            key = lax.broadcasted_iota(jnp.int32, (end, ROWS), 0)
            allowed = (key <= query) & (key >= lowest)
            q, d = r.q[rows, lanes], r.datt[rows, lanes]
            k, v = r.k[0:end, lanes], r.v[0:end, lanes]
            dq = jnp.zeros((ROWS, 128), jnp.float32)
            for side in range(2):
                mine = (lax.div(lane, 64) == side).astype(jnp.float32).astype(jnp.bfloat16)
                q_own, d_own = q * mine, d * mine
                scores = dot(k, q_own, NT) * 0.125
                lse = self.lse[l, pair * 2 + side : pair * 2 + side + 1, rows]
                probs = jnp.where(allowed, jnp.exp(scores - lse), 0.0)
                dprob = dot(v, d_own, NT)
                centre = jnp.sum(probs * dprob, axis=0, keepdims=True)
                dscore = (probs * (dprob - centre)).astype(jnp.bfloat16)
                r.dv[0:end] = r.dv[0:end] + dot(probs.astype(jnp.bfloat16), d_own, NN)
                r.dk[0:end] = r.dk[0:end] + dot(dscore, q_own, NN)
                dq = dq + dot(dscore, k * mine, TN)
            r.dqkv[0, rows, lanes] = (dq * 0.125).astype(jnp.bfloat16)
        if turn == 1:
            r.dqkv[1, :, lanes] = (r.dk[...] * 0.125).astype(jnp.bfloat16)
            r.dqkv[2, :, lanes] = r.dv[...].astype(jnp.bfloat16)

    def small_swap(self, step):
        r = self.refs
        z = self.z
        to = (
            self.dp + self.step_x,
            self.dp + self.step_y,
            self.dp + 4 - 8 * lax.rem(z, 2),
            self.dp + 8 - 16 * lax.div(z, 2),
        )[step]
        return self.copy(
            r.small, r.small_in.at[step], r.small_s.at[step], r.small_r.at[step], (to, self.core)
        )

    def small_stage(self, step):
        if step > 0:
            copy = self.small_swap(step - 1)
            copy.wait_send()
            copy.wait_recv()
            self.refs.small[...] = self.refs.small[...] + self.refs.small_in[step - 1]
        if step < 4:
            self.small_swap(step).start()

    def run(self):
        r = self.refs
        pltpu.make_async_copy(self.cotangent, r.low, r.cot_s).start()
        self.fetch(ACT, 1)
        r.small[...] = jnp.zeros(r.small.shape, jnp.float32)
        far = (self.dp + 8 - 16 * lax.div(self.z, 2), self.core)
        self.barrier(((self.dp, 1 - self.core), far))

        def step(t, carry):
            l = 1 - lax.div(t, PIECES)
            for p in range(PIECES):
                @pl.when((lax.rem(t, PIECES) == p) & (t < 2 * PIECES))
                def _():
                    self.piece(p, l)

            for s in range(5):
                @pl.when(t == 2 * PIECES + s)
                def _():
                    self.small_stage(s)

            self.tick(t)
            return carry

        lax.fori_loop(0, self.ticks, step, 0)
        pltpu.make_async_copy(r.low, self.grad_tokens, r.tokens_s).wait()
        self.small_out[...] = r.small[...]


def backward(kept, weights, gain, lse, positions, cotangent, slots=6, lags=(4, 2, 2, 2, 2, 2, 2, 2, 4)):
    D = cotangent.shape[1]
    _, T, W = kept[1].shape
    jobs = 2 * PER_LAYER
    plan = Backward(2 * jobs, UNIT // 2, UNIT, slots, lags)
    plan.T, plan.D, plan.W, plan.F = T, D, W, weights[0].shape[1]
    scratch = plan.scratch() | plan.more_scratch()
    n = len(kept)

    def kernel(*refs):
        layers = [[ref.at[i] for i in range(2)] for ref in refs[:n]]
        norm1, q, k, v, att, h_mid, norm2, pre, act, h = layers
        plan.inputs = dict(zip(plan.LOADS, (act, pre, list(zip(norm1, norm2)), list(zip(h, h_mid)), att, q, k, v)))
        for name, weight in zip((W_SHRINK, W_EXPAND, W_MERGE, W_HEADS), refs[n : n + 4]):
            plan.inputs[name] = [weight.at[i] for i in range(2)]
        plan.cotangent, plan.gain, plan.lse, plan.positions = refs[n + 4 : n + 8]
        plan.target, plan.source, plan.grad_tokens, plan.small_out = refs[n + 8 : n + 12]
        plan.setup(SimpleNamespace(**dict(zip(scratch, refs[n + 12 :]))))
        plan.run()

    hbm = pl.BlockSpec(memory_space=pl.ANY)
    vmem = pl.BlockSpec(memory_space=pltpu.VMEM)
    flat = jax.ShapeDtypeStruct((jobs, 2, UNIT, UNIT), jnp.float32)
    target, _, grad_tokens, small = pl.pallas_call(
        kernel,
        out_shape=(
            flat,
            flat,
            jax.ShapeDtypeStruct((T, D), jnp.bfloat16),
            jax.ShapeDtypeStruct((2 * SMALL, D), jnp.float32),
        ),
        in_specs=[hbm] * (n + 5) + [vmem] * 3,
        out_specs=(hbm, hbm, hbm, vmem),
        scratch_shapes=list(scratch.values()),
        compiler_params=pltpu.CompilerParams(
            collective_id=0, has_side_effects=True, vmem_limit_bytes=61 * 2**20
        ),
    )(*kept, *weights, cotangent, gain, lse, positions)
    return target, grad_tokens, small


def gelu(x):
    return 0.5 * x * (1.0 + jnp.tanh(0.7978845608028654 * (x + 0.044715 * x * x * x)))


class Forward:
    KEPT = (NORM1, Q, K, V, ATT, H_MID, NORM2, PRE, ACT, H)

    WEIGHTS = (HEADS, MERGE, EXPAND, SHRINK)

    def scratch(self):
        T, D, W, F = self.T, self.D, self.W, self.F
        low, full = jnp.bfloat16, jnp.float32
        dma = pltpu.SemaphoreType.DMA
        n = T // ROWS
        return dict(
            norm1=pltpu.VMEM((T, D), low), q=pltpu.VMEM((T, W), low), k=pltpu.VMEM((T, W), low), v=pltpu.VMEM((T, W), low),
            att=pltpu.VMEM((T, W), low), h_mid=pltpu.VMEM((T, D), full), norm2=pltpu.VMEM((T, D), low),
            pre=pltpu.VMEM((T, F), full), act=pltpu.VMEM((T, F), low), h=pltpu.VMEM((T, D), full),
            low=pltpu.VMEM((T, D), low), part=pltpu.VMEM((2, T, D), full), came=pltpu.VMEM((2, T, D), full),
            bias=pltpu.VMEM((n, ROWS, T), full),
            heads=pltpu.VMEM((2, 3, D, W), low), merge=pltpu.VMEM((2, W, D), low),
            expand=pltpu.VMEM((2, D, F), low), shrink=pltpu.VMEM((2, F, D), low),
            kept_s=dma((len(self.KEPT), n)), weight_s=dma((4, 2)), token_s=dma, out_s=dma((n,)),
            core_s=dma((2, n)), core_r=dma((2, n)),
        )

    def rows(self, b):
        return pl.ds(pl.multiple_of(b * ROWS, ROWS), ROWS)

    def keep_copy(self, name, l, b):
        at = self.rows(b)
        return pltpu.make_async_copy(
            getattr(self.refs, name).at[at], self.kept[name].at[l, at], self.refs.kept_s.at[self.KEPT.index(name), b]
        )

    def free(self, l, b, *names):
        @pl.when(l == 1)
        def _():
            for name in names:
                self.keep_copy(name, 0, b).wait()

    def keep(self, l, b, *names):
        for name in names:
            self.keep_copy(name, l, b).start()

    def weight_copy(self, name, l):
        at = self.WEIGHTS.index(name)
        return pltpu.make_async_copy(self.weights[name].at[l], getattr(self.refs, name).at[l], self.refs.weight_s.at[at, l])

    def core_copy(self, kind, b):
        r, at = self.refs, self.rows(b)
        return pltpu.make_async_remote_copy(
            src_ref=r.part.at[kind, at], dst_ref=r.came.at[kind, at],
            send_sem=r.core_s.at[kind, b], recv_sem=r.core_r.at[kind, b],
            device_id=(lax.axis_index("dp"), 1 - lax.axis_index("tensor")), device_id_type=MESH,
        )

    def summed(self, kind, b):
        copy = self.core_copy(kind, b)
        copy.wait_send()
        copy.wait_recv()
        at = self.rows(b)
        return self.refs.part[kind, at] + self.refs.came[kind, at]

    def norm(self, x, l, which):
        xhat, _ = norm_parts(x)
        return (xhat * self.gain[l, which : which + 1] + self.shift[l, which : which + 1]).astype(jnp.bfloat16)

    def first(self, l, b):
        r, at = self.refs, self.rows(b)
        W = self.W
        self.free(l, b, H)

        @pl.when(l == 0)
        def _():
            r.h[at] = r.low[at].astype(jnp.float32)

        @pl.when(l == 1)
        def _():
            r.h[at] = r.h_mid[at] + (self.summed(1, b) + self.branch[0, 1:2])

        self.free(l, b, NORM1, Q, K, V, ATT)
        low = self.norm(r.h[at], l, 0)
        r.norm1[at] = low
        r.q[at] = (dot(low, r.heads[l, 0], NN) + self.offsets[l, 0:1]).astype(jnp.bfloat16)
        r.k[at] = dot(low, r.heads[l, 1], NN).astype(jnp.bfloat16)
        r.v[at] = (dot(low, r.heads[l, 2], NN) + self.offsets[l, 1:2]).astype(jnp.bfloat16)
        for i in range(self.T // ROWS):
            @pl.when(b == i)
            def _():
                self.attend(l, i)

        r.part[0, at] = dot(r.att[at], r.merge[l], NN)
        self.core_copy(0, b).start()
        self.keep(l, b, H, NORM1, Q, K, V, ATT)

    def attend(self, l, b):
        r = self.refs
        rows, end = slice(b * ROWS, (b + 1) * ROWS), (b + 1) * ROWS

        @pl.when(l == 0)
        def _():
            query = b * ROWS + lax.broadcasted_iota(jnp.int32, (ROWS, 1), 0)
            spread = jnp.concatenate([self.positions[...].astype(jnp.float32)] * 16, axis=0).T
            column = jnp.concatenate([spread[:, j : j + 1] for j in range(2 * b, 2 * b + 2)], axis=0)
            lowest = query - column.astype(jnp.int32)
            key = lax.broadcasted_iota(jnp.int32, (ROWS, end), 1)
            r.bias[b, :, 0:end] = jnp.where((key <= query) & (key >= lowest), 0.0, -1e30)

        lane = lax.broadcasted_iota(jnp.int32, (1, 128), 1)
        logs = jnp.zeros((ROWS, 128), jnp.float32)
        for pair in range(self.W // 128):
            lanes = slice(pair * 128, (pair + 1) * 128)
            q, k, v = r.q[rows, lanes], r.k[0:end, lanes], r.v[0:end, lanes]
            total = jnp.zeros((ROWS, 128), jnp.float32)
            for side in range(2):
                mine = (lax.div(lane, 64) == side).astype(jnp.float32)
                scores = dot(q * (mine * 0.125).astype(jnp.bfloat16), k, NT) + r.bias[b, :, 0:end]
                highest = jnp.max(scores, axis=-1, keepdims=True)
                weights = jnp.exp(scores - highest)
                amount = jnp.sum(weights, axis=-1, keepdims=True)
                probs = (weights * (1.0 / amount)).astype(jnp.bfloat16)
                total = total + dot(probs, v * mine.astype(jnp.bfloat16), NN)
                logs = jnp.where(lane == pair * 2 + side, highest + jnp.log(amount), logs)
            r.att[rows, lanes] = total.astype(jnp.bfloat16)
        self.lse[l, :, rows] = logs.T[0:8]

    def second(self, l, b):
        r, at = self.refs, self.rows(b)
        self.free(l, b, H_MID, NORM2, PRE, ACT)
        middle = r.h[at] + (self.summed(0, b) + self.branch[l, 0:1])
        r.h_mid[at] = middle
        low = self.norm(middle, l, 1)
        r.norm2[at] = low
        for c in range(0, self.F, 512):
            pre = dot(low, r.expand[l, :, c : c + 512], NN) + self.hidden[pl.ds(l, 1), c : c + 512]
            r.pre[at, c : c + 512] = pre
            r.act[at, c : c + 512] = gelu(pre).astype(jnp.bfloat16)
        r.part[1, at] = dot(r.act[at], r.shrink[l], NN)
        self.core_copy(1, b).start()
        self.keep(l, b, H_MID, NORM2, PRE, ACT)

    def finish(self, b):
        r, at = self.refs, self.rows(b)
        r.low[at] = (r.h_mid[at] + (self.summed(1, b) + self.branch[1, 1:2])).astype(jnp.bfloat16)
        pltpu.make_async_copy(r.low.at[at], self.output.at[at], r.out_s.at[b]).start()

    def run(self):
        r = self.refs
        n = self.T // ROWS
        load = pltpu.make_async_copy(self.tokens, r.low, r.token_s)
        load.start()
        for name in self.WEIGHTS:
            self.weight_copy(name, 0).start()
        other = (lax.axis_index("dp"), 1 - lax.axis_index("tensor"))
        bar = pltpu.get_barrier_semaphore()
        pl.semaphore_signal(bar, inc=1, device_id=other, device_id_type=MESH)
        pl.semaphore_wait(bar, 1)
        load.wait()

        def turn(t, carry):
            for l in range(2):
                @pl.when(t == l * n)
                def _():
                    self.weight_copy(HEADS, l).wait()
                    self.weight_copy(MERGE, l).wait()

            @pl.when(t < 2 * n)
            def _():
                self.first(lax.div(t, n), lax.rem(t, n))

            for l in range(2):
                @pl.when(t == l * n + 1)
                def _():
                    self.weight_copy(EXPAND, l).wait()
                    self.weight_copy(SHRINK, l).wait()

            @pl.when(t == 1)
            def _():
                for name in self.WEIGHTS:
                    self.weight_copy(name, 1).start()

            @pl.when((t >= 1) & (t < 2 * n + 1))
            def _():
                self.second(lax.div(t - 1, n), lax.rem(t - 1, n))

            @pl.when(t >= n + 2)
            def _():
                self.finish(t - n - 2)

            return carry

        lax.fori_loop(0, 2 * n + 2, turn, 0)
        for b in range(n):
            for name in self.KEPT:
                self.keep_copy(name, 1, b).wait()
            pltpu.make_async_copy(r.low.at[self.rows(b)], self.output.at[self.rows(b)], r.out_s.at[b]).wait()


def forward(tokens, positions, weights, rows):
    plan = Forward()
    T, D = tokens.shape
    plan.T, plan.D, plan.W, plan.F = T, D, weights[0].shape[3], weights[2].shape[2]
    scratch = plan.scratch()
    kinds = plan.KEPT

    def kernel(tokens, heads, merge, expand, shrink, positions, gain, shift, offsets, branch, hidden, output, lse, *refs):
        plan.tokens, plan.positions, plan.output, plan.lse = tokens, positions, output, lse
        plan.weights = dict(zip(plan.WEIGHTS, (heads, merge, expand, shrink)))
        plan.gain, plan.shift, plan.offsets, plan.branch, plan.hidden = gain, shift, offsets, branch, hidden
        plan.kept = dict(zip(kinds, refs))
        plan.refs = SimpleNamespace(**dict(zip(scratch, refs[len(kinds) :])))
        plan.run()

    hbm = pl.BlockSpec(memory_space=pl.ANY)
    vmem = pl.BlockSpec(memory_space=pltpu.VMEM)
    kept_shapes = [jax.ShapeDtypeStruct((2,) + scratch[name].shape, scratch[name].dtype) for name in kinds]
    out = pl.pallas_call(
        kernel,
        out_shape=[jax.ShapeDtypeStruct((T, D), jnp.bfloat16), jax.ShapeDtypeStruct((2, 8, T), jnp.float32)] + kept_shapes,
        in_specs=[hbm] * 5 + [vmem] * 6,
        out_specs=[hbm, vmem] + [hbm] * len(kept_shapes),
        scratch_shapes=list(scratch.values()),
        compiler_params=pltpu.CompilerParams(
            collective_id=1, has_side_effects=True, vmem_limit_bytes=61 * 2**20
        ),
    )(tokens, *weights, positions, *rows)
    return out[0], out[1], out[2:]


def spread(flat, small, shapes, dtype=jnp.float32):
    half = flat.shape[0] // 2
    width = small.shape[1]

    def kernel(source, sums, gain, shift, heads, offsets, merge, branch, expand, hidden, shrink, held, into, out):
        loads, copies = [], []

        def put(g, u, target):
            i = len(copies)
            loads.append(pltpu.make_async_copy(source.at[g, u], held.at[i], into.at[i]))
            copies.append(pltpu.make_async_copy(held.at[i], target, out.at[i]))
            loads[-1].start()

        for l in range(2):
            base = (1 - l) * half
            for u in range(2):
                rows = pl.ds(u * UNIT, UNIT)
                for i in range(4):
                    at = pl.ds((i // 2) * 2 * UNIT + u * UNIT, UNIT)
                    put(base + i, u, shrink.at[l, at, pl.ds((i % 2) * UNIT, UNIT)])
                    put(base + 4 + i, u, expand.at[l, rows, pl.ds(i * UNIT, UNIT)])
                put(base + 8, u, merge.at[l, :, rows])
                for c in range(3):
                    put(base + 9 + c, u, heads.at[l, c, rows])
            for target, at in ((gain, GAIN), (shift, SHIFT), (branch, BRANCH)):
                target[l] = sums[l * SMALL + at : l * SMALL + at + 2]
            for i in range(2):
                at = l * SMALL + HIDDEN + i
                hidden[l : l + 1, i * width : (i + 1) * width] = sums[at : at + 1]
                at = l * SMALL + OFFSETS
                offsets[l, i : i + 1] = sums[at : at + 1, i * UNIT : (i + 1) * UNIT]
        for load, copy in zip(loads, copies):
            load.wait()
            copy.start()
        for copy in copies:
            copy.wait()

    hbm = pl.BlockSpec(memory_space=pl.ANY)
    vmem = pl.BlockSpec(memory_space=pltpu.VMEM)
    return pl.pallas_call(
        kernel,
        out_shape=[jax.ShapeDtypeStruct(s, dtype) for s in shapes],
        in_specs=[hbm, vmem],
        out_specs=[vmem, vmem, hbm, vmem, hbm, vmem, hbm, vmem, hbm],
        scratch_shapes=[
            pltpu.VMEM((2 * flat.shape[0], UNIT, UNIT), dtype),
            pltpu.SemaphoreType.DMA((2 * flat.shape[0],)),
            pltpu.SemaphoreType.DMA((2 * flat.shape[0],)),
        ],
        compiler_params=pltpu.CompilerParams(has_side_effects=True, vmem_limit_bytes=48 * 2**20),
    )(flat, small)


def on_device(
    tokens,
    positions,
    norm_gain,
    norm_shift,
    heads_weight,
    offsets,
    merge_weight,
    branch_bias,
    expand_weight,
    hidden_bias,
    shrink_weight,
    cotangent,
):
    rows = (norm_gain, norm_shift, offsets, branch_bias, hidden_bias)
    places = positions.reshape(-1, 128)
    output, lse, kept = forward(
        tokens, places, (heads_weight, merge_weight, expand_weight, shrink_weight), rows
    )
    flat, grad_tokens, small = backward(
        kept, (shrink_weight, expand_weight, merge_weight, heads_weight), norm_gain, lse, places, cotangent
    )
    ranks = lax.axis_size("dp")
    if ranks > BLOCK:
        groups = [[j * BLOCK + i for j in range(ranks // BLOCK)] for i in range(BLOCK)]
        flat, small = lax.psum((flat, small), "dp", axis_index_groups=groups)
    shapes = [norm_gain, norm_shift, heads_weight, offsets, merge_weight, branch_bias, expand_weight, hidden_bias, shrink_weight]
    return (output, grad_tokens, *spread(flat, small, [like.shape for like in shapes]))


def solution(mesh):
    placed = (
        P("dp", None),
        P("dp"),
        P(),
        P(),
        P(None, None, None, "tensor"),
        P(None, None, "tensor"),
        P(None, "tensor", None),
        P(),
        P(None, None, "tensor"),
        P(None, "tensor"),
        P(None, "tensor", None),
        P("dp", None),
    )
    return jax.shard_map(
        on_device,
        mesh=mesh,
        in_specs=placed,
        out_specs=(
            P("dp", None),
            P("dp", None),
            P(),
            P(),
            P(None, None, None, "tensor"),
            P(None, None, "tensor"),
            P(None, "tensor", None),
            P(),
            P(None, None, "tensor"),
            P(None, "tensor"),
            P(None, "tensor", None),
        ),
        check_vma=False,
    )
```

time: 745 us -> 494 us (0.66)
  local copies, waits for them, and re-layouts: 143 us -> 3.99 us
  Pallas kernels: 402 us -> 480 us
  waiting for transfers between devices: 66.6 us -> 0 us
  matrix products: 60.1 us -> 0 us
  other arithmetic: 50.7 us -> 0 us
  between operations: 14.7 us -> 1.07 us
    pallas_call x0 -> x2, Pallas kernels: none -> 78.1 us  [the longest x1 57.7 us: forward(): pl.pallas_call(kernel, out_shape=[jax.ShapeDtypeStruct((T, D), jnp.bfloat...]
    psum x4 -> x0, waiting for transfers between devices: 66.6 us -> none  [add_branch(): return stream + (lax.psum(partial_sum, 'tensor') + bias_row)]
    dot_general x16 -> x0, matrix products: 60.1 us -> none  [the longest x4 17.7 us: one_block(): jnp.einsum('hqk,khd->qhd', chances, value_rows, preferred_element_type=jn...]
    reshape x7 -> x0, local copies, waits for them, and re-layouts: 47.6 us -> none  [the longest x2 30.3 us: on_device(): flat[:, 0:4].reshape(LAYERS, 2, 2, 2, UNIT, UNIT)]
    slice x18 -> x0, local copies, waits for them, and re-layouts: 45.9 us -> none  [the longest x2 19.2 us: on_device(): flat[:, 0:4].reshape(LAYERS, 2, 2, 2, UNIT, UNIT)]
    reduce_sum x12 -> x0, other arithmetic: 27.6 us -> none  [the longest x4 14.5 us: one_block(): totals = jnp.sum(weights, axis=-1, keepdims=True)]
    convert_element_type x12 -> x0, other arithmetic: 20 us -> none  [the longest x4 8.87 us: on_device(): value_rows = (projected[2] + offsets[layer_index, 1]).astype(jnp.bfloat16)]
    transpose x2 -> x0, local copies, waits for them, and re-layouts: 17.8 us -> none  [on_device(): expand = flat[:, 4:8].transpose(0, 2, 3, 1, 4).reshape(expand_weight.shape)]
  transfers between devices with their start and end apart: 4 -> 0, of which waited for: 3 -> 0; matrix products, arithmetic and copies ran while one was open for 16% -> 0% of each run, Pallas kernels for 54% -> 0%
where the time goes in v3:
time: 494 us; the launch traced here: 485 us
  Pallas kernels  480 us (97%)
    pallas_call x1, Pallas kernels, backward(): pl.pallas_call(kernel, out_shape=(flat, flat, jax.ShapeDtypeStruct((T, D)...  401 us
    pallas_call x1, Pallas kernels, forward(): pl.pallas_call(kernel, out_shape=[jax.ShapeDtypeStruct((T, D), jnp.bfloat...  57.7 us
    pallas_call x1, Pallas kernels, spread(): pl.pallas_call(kernel, out_shape=[jax.ShapeDtypeStruct(s, dtype) for s in...  20.4 us

profile of v3, /device:TPU:0, one launch (start us, length us, event | category | flops | bytes accessed | tf_op | source)
XLA Modules:
  0.0 484.6 jit_solution(17628486455643395291)
XLA Ops:
  0.6 57.7 %shard_map.203 = (bf16[1024,768]{1,0:T(8,128)(2,1)}, f32[2,8,1024]{2,1,0:T(8,128)}, bf16[2,1024,768]{2,1,0:T(8,128)(2,1)}, bf16[2,1024,384]{2,1,0:T(8,128)(2,1)}...) custom-call(bf16[1024,768]{1,0:T(8,128)(2,1)} %tokens.1, ...), custom_call_target="tpu_custom_call" | custom-call | tf_op jit(solution)/shard_map/pallas_call | solution.py:969
  58.4 401.5 %shard_map.204 = (f32[24,2,384,384]{3,2,1,0:T(8,128)}, f32[24,2,384,384]{3,2,1,0:T(8,128)}, bf16[1024,768]{1,0:T(8,128)(2,1)}, f32[32,768]{1,0:T(8,128)}) custom-call(bf16[2,1024,768]{2,1,0:T(8,128)(2,1)} %get-tuple-element.36.refs_0_, bf16[2,1024,384]{2,1,0:T(8,128)(2,1)} %get-tuple-element.37.refs_1_, bf16[2,1024,384]{2,1,0:T(8,128)(2,1)} %get-tuple-element.38.refs_2_, ...), custom_call_target="tpu_custom_call" | custom-call | tf_op jit(solution)/shard_map/pallas_call | solution.py:734
  459.8 0.0 copy-start
  459.8 0.9 copy-done
  460.7 0.0 copy-start.1
  460.7 20.4 %shard_map.205 = (f32[2,2,768]{2,1,0:T(2,128)}, f32[2,2,768]{2,1,0:T(2,128)}, f32[2,3,768,384]{3,2,1,0:T(8,128)}, f32[2,2,384]{2,1,0:T(2,128)}, f32[2,384,768]{2...) custom-call(f32[24,2,384,384]{3,2,1,0:T(8,128)} %get-tuple-element.4, ...), custom_call_target="tpu_custom_call" | custom-call | tf_op jit(solution)/shard_map/pallas_call | solution.py:1021
  481.1 0.0 copy-start.2
  481.2 0.0 copy-done.1
  481.2 1.1 copy.25
  482.3 0.8 copy-done.2
  483.1 1.1 copy.26
Async XLA Ops:
  459.8 0.9 copy-start
  460.7 20.4 %copy-start.1 = (bf16[1024,768]{1,0:T(8,128)(2,1)S(1)}, bf16[1024,768]{1,0:T(8,128)(2,1)}, u32[]{:S(2)}) copy-start(bf16[1024,768]{1,0:T(8,128)(2,1)} %get-tuple-element.70) | copy-start | bytes 4718596
  481.1 2.0 copy-start.2
